TPU v7x, 32 devices: a whole 2x2x4 slice. The times are simulated.
32 devices in a mesh: blk: 8 (over z, y), rep: 4 (over x, core).
Axes of the slice: x: 2, y: 2, z: 4, core: 2. Of those that a mesh axis runs over, the one named last changes fastest.
Arguments:
- users: bfloat16 [32768, 128], P(('blk', 'rep')), may hold values from -2 to 2
- items: bfloat16 [8192, 128], P('blk'), may hold values from -2 to 2
- ratings: bfloat16 [8, 4, 3, 40, 128, 128], P('blk', 'rep'), may hold values from 0 to 4
- user_tiles: int32 [8, 4, 3, 40], P('blk', 'rep'), may hold values from 0 to 7
- item_tiles: int32 [8, 4, 3, 40], P('blk', 'rep'), may hold values from 0 to 7
- counts: int32 [8, 4, 3], P('blk', 'rep'), may hold values from 5 to 40, as said below
Outputs:
- user_new: bfloat16 [32768, 128], P(('blk', 'rep'))
- item_new: bfloat16 [8192, 128], P('blk')
Inputs may be any that keep to these rules, and one draw needn't show every extreme that they name: `counts`: each device and stop has between 5 and 40 live slots, the first ones of its list; some device has all 40 live for some stop.
All inputs are finite; a program needn't handle non-finite values.
Results may differ from a plain program's by a relative error of at most 0.0033.
Values may be sent and summed in bfloat16 or wider, within the bound.
No kernel may reach another device: no remote copies, remote signals or barrier semaphores. Data moves between devices by JAX's collectives and lax.ppermute only.
A program may use at most 64 MiB of HBM per device.

v0:
```python
import math

import jax
import jax.numpy as jnp
from jax import lax
from jax.sharding import PartitionSpec as P

confidence = 0.5
shrinkage = 0.05
step_gain = 0.3
slot_group = 8


def shifted(block, axis, distance):
    devices = range(lax.axis_size(axis))
    route = [((i - distance) % len(devices), i) for i in devices]
    return lax.ppermute(block, axis, route)


def on_device(users, items, ratings, user_tiles, item_tiles, counts):
    tile_size = ratings.shape[-1]
    rank_width = users.shape[1]
    stations = ratings.shape[2]
    slots_all = ratings.shape[3]
    user_count = users.shape[0] // tile_size
    item_count = items.shape[0] // tile_size
    user_blocks = users.reshape(user_count, tile_size, rank_width)
    user_ids = jnp.arange(user_count, dtype=jnp.int32)
    item_ids = jnp.arange(item_count, dtype=jnp.int32)
    group_slots = jnp.arange(slot_group, dtype=jnp.int32)
    grad_user = jnp.zeros((user_count, tile_size, rank_width), jnp.float32)
    current = items
    partials = []
    for station in range(stations):
        if station > 0:
            current = shifted(current, "blk", -1)
        item_blocks = current.reshape(item_count, tile_size, rank_width)
        live_count = counts[0, 0, station]
        groups = (live_count + slot_group - 1) // slot_group
        stop_users = user_tiles[0, 0, station]
        stop_items = item_tiles[0, 0, station]
        stop_ratings = ratings[0, 0, station]

        def group_step(
            group_index,
            totals,
            item_blocks=item_blocks,
            live_count=live_count,
            stop_users=stop_users,
            stop_items=stop_items,
            stop_ratings=stop_ratings,
        ):
            user_acc, item_acc = totals
            first_slot = group_index * slot_group
            user_pick = lax.dynamic_slice_in_dim(stop_users, first_slot, slot_group)
            item_pick = lax.dynamic_slice_in_dim(stop_items, first_slot, slot_group)
            rating_tiles = lax.dynamic_slice_in_dim(stop_ratings, first_slot, slot_group, 0)
            valid_slots = (first_slot + group_slots < live_count).astype(jnp.float32)
            user_rows = user_blocks[user_pick]
            item_rows = item_blocks[item_pick]
            predicted = jnp.einsum(
                "gak,gbk->gab", user_rows, item_rows, preferred_element_type=jnp.float32
            )
            rating_vals = rating_tiles.astype(jnp.float32)
            residual = (
                (1.0 + confidence * rating_vals)
                * (rating_vals - predicted)
                * valid_slots[:, None, None]
            ).astype(jnp.bfloat16)
            user_terms = jnp.einsum(
                "gab,gbk->gak", residual, item_rows, preferred_element_type=jnp.float32
            )
            item_terms = jnp.einsum(
                "gab,gak->gbk", residual, user_rows, preferred_element_type=jnp.float32
            )
            user_onehot = (user_pick[:, None] == user_ids[None, :]).astype(jnp.float32)
            item_onehot = (item_pick[:, None] == item_ids[None, :]).astype(jnp.float32)
            user_acc = user_acc + jnp.einsum(
                "gn,gak->nak", user_onehot, user_terms, precision=lax.Precision.HIGHEST
            )
            item_acc = item_acc + jnp.einsum(
                "gn,gak->nak", item_onehot, item_terms, precision=lax.Precision.HIGHEST
            )
            return (user_acc, item_acc)

        item_zero = jnp.zeros((item_count, tile_size, rank_width), jnp.float32)
        grad_user, item_grad = lax.fori_loop(0, groups, group_step, (grad_user, item_zero))
        partials.append(item_grad.reshape(items.shape[0], rank_width))
    rep_count = lax.axis_size("rep")
    rate_user = step_gain / math.sqrt(stations * slots_all * tile_size * tile_size / users.shape[0])
    rate_item = step_gain / math.sqrt(
        rep_count * stations * slots_all * tile_size * tile_size / items.shape[0]
    )
    users32 = users.astype(jnp.float32)
    items32 = items.astype(jnp.float32)
    user_new = users32 - rate_user * (grad_user.reshape(users.shape) + shrinkage * users32)
    item_sum = partials[0]
    for station in range(1, stations):
        item_sum = item_sum + shifted(partials[station], "blk", station)
    item_sum = lax.psum(item_sum, "rep")
    item_new = (items32 - rate_item * (item_sum + shrinkage * items32)).astype(jnp.bfloat16)
    return (user_new.astype(jnp.bfloat16), item_new)


def solution(mesh):
    return jax.shard_map(
        on_device,
        mesh=mesh,
        in_specs=(
            P(("blk", "rep"), None),
            P("blk", None),
            P("blk", "rep", None, None, None, None),
            P("blk", "rep", None, None),
            P("blk", "rep", None, None),
            P("blk", "rep", None),
        ),
        out_specs=(P(("blk", "rep"), None), P("blk", None)),
        check_vma=False,
    )
```

profile of v0, /device:TPU:0, one launch (start us, length us, event | category | flops | bytes accessed | tf_op | source)
XLA Modules:
  0.0 145.3 jit_solution(7419626492696536287)
XLA Ops:
  7.2 6.1 %collective-permute-start = (bf16[1024,128]{1,0:T(8,128)(2,1)}, bf16[1024,128]{1,0:T(8,128)(2,1)}, u32[]{:S(2)}, u32[]{:S(2)}) collective-permute-start(bf16[1024,128]{1,0:T(8,128)(2,1)} %param.13), channel_id=1, source_target_pairs={{4,0},{8,4},{12,8},{16,12},{20,16},{24,20},{28,24},{0,28},{5,1},{9... | collective-permute-start | bytes 786440 | tf_op jit(solution)/shard_map/ppermute | solution.py:17
  13.3 1.4 fusion.49
  15.4 4.1 %slice_bitcast_fusion = (bf16[40,128,128]{2,1,0:T(8,128)(2,1)}, bf16[40,128,128]{2,1,0:T(8,128)(2,1)S(1)}, bf16[40,128,128]{2,1,0:T(8,128)(2,1)}) fusion(bf16[1,1,3,40,128,128]{5,4,3,2,1,0:T(8,128)(2,1)} %param.14), kind=kLoop, calls=%fused_computation.75 | loop fusion | bytes 7864320 | tf_op jit(solution)/shard_map/squeeze | solution.py:42
  19.7 12.8 %while.45 = (s32[]{:T(128)}, f32[8,128,128]{2,0,1:T(8,128)S(1)}, f32[8,128,128]{2,0,1:T(8,128)S(1)}, s32[]{:T(128)}, s32[40]{0:T(128)S(1)}, /*index=5*/bf16[40,1...) while((s32[]{:T(128)}, f32[8,128,128]{2,0,1:T(8,128)S(1)}, ...), condition=%wide.region_1.2_spmd.clone.clone, body=%wide.region_0.1_spmd.clone.clone.sunk | while | flops 127011024 | bytes 7348867 | solution.py:87
  19.8 0.6 gather_fusion
  20.4 0.6 gather_fusion.1
  21.0 0.7 compare_convert_fusion.6
  22.3 0.7 convolution_add_fusion.13
  23.2 0.7 convolution_add_fusion.12
  24.0 0.6 gather_fusion
  24.7 0.6 gather_fusion.1
  25.3 0.7 compare_convert_fusion.6
  26.5 0.7 convolution_add_fusion.13
  27.5 0.7 convolution_add_fusion.12
  28.3 0.6 gather_fusion
  28.9 0.6 gather_fusion.1
  29.5 0.7 compare_convert_fusion.6
  30.8 0.7 convolution_add_fusion.13
  31.7 0.7 convolution_add_fusion.12
  33.9 12.2 %while.46 = (s32[]{:T(128)}, f32[8,128,128]{2,0,1:T(8,128)S(1)}, f32[8,128,128]{2,0,1:T(8,128)S(1)}, s32[]{:T(128)}, s32[40]{0:T(128)S(1)}, /*index=5*/bf16[40,1...) while((s32[]{:T(128)}, f32[8,128,128]{2,0,1:T(8,128)S(1)}, ...), condition=%wide.region_3.4_spmd.clone.clone, body=%wide.region_2.3_spmd.clone.clone.sunk | while | flops 127011024 | bytes 7348867 | solution.py:87
  34.0 0.6 gather_fusion.2
  34.6 1.5 %gather_fusion.3 = bf16[8,128,128]{2,1,0:T(8,128)(2,1)S(1)} fusion(bf16[8,128,128]{2,1,0:T(8,128)(2,1)} %get-tuple-element.833, s32[1024]{0:T(1024)S(1)} %pad_clamp_fusion.15), kind=kCustom, calls=%fused_computation.3.clone.clone.1 | custom fusion | bytes 524320 | tf_op jit(solution)/shard_map/while/body/gather | solution.py:60
  36.8 1.3 fusion.136
  38.3 0.7 convolution_add_fusion.15
  39.3 0.7 convolution_add_fusion.14
  40.1 0.6 gather_fusion.2
  40.7 1.5 %gather_fusion.3 = bf16[8,128,128]{2,1,0:T(8,128)(2,1)S(1)} fusion(bf16[8,128,128]{2,1,0:T(8,128)(2,1)} %get-tuple-element.833, s32[1024]{0:T(1024)S(1)} %pad_clamp_fusion.15), kind=kCustom, calls=%fused_computation.3.clone.clone.1 | custom fusion | bytes 524320 | tf_op jit(solution)/shard_map/while/body/gather | solution.py:60
  42.9 1.3 fusion.136
  44.4 0.7 convolution_add_fusion.15
  45.4 0.7 convolution_add_fusion.14
  46.2 20.3 %collective-permute-start.2 = (f32[1024,128]{1,0:T(8,128)S(1)}, f32[1024,128]{1,0:T(8,128)}, u32[]{:S(2)}, u32[]{:S(2)}) collective-permute-start(f32[1024,128]{1,0:T(8,128)S(1)} %bitcast.122), channel_id=1, source_target_pairs={{28,0},{0,4},{4,8},{8,12},{12,16},{16,20},{20,24},{24,28},{29,1},{... | collective-permute-start | bytes 1572872 | tf_op jit(solution)/shard_map/ppermute | solution.py:17
  66.6 26.3 %while.47 = (s32[]{:T(128)}, f32[8,128,128]{2,0,1:T(8,128)S(1)}, f32[8,128,128]{2,0,1:T(8,128)S(1)}, s32[]{:T(128)}, s32[40]{0:T(128)S(1)}, /*index=5*/bf16[40,1...) while((s32[]{:T(128)}, f32[8,128,128]{2,0,1:T(8,128)S(1)}, ...), condition=%wide.region_5.6_spmd.clone.clone, body=%wide.region_4.5_spmd.clone.clone.sunk | while | flops 127011024 | bytes 7348867 | solution.py:87
  66.7 0.6 gather_fusion.4
  67.3 0.6 gather_fusion.5
  67.9 0.7 compare_convert_fusion.8
  68.6 1.3 fusion.149
  70.2 0.7 convolution_add_fusion.17
  71.1 0.7 convolution_add_fusion.16
  72.0 0.6 gather_fusion.4
  72.6 0.6 gather_fusion.5
  73.2 0.7 compare_convert_fusion.8
  73.9 1.3 fusion.149
  75.5 0.7 convolution_add_fusion.17
  76.4 0.7 convolution_add_fusion.16
  77.2 0.6 gather_fusion.4
  78.5 0.7 compare_convert_fusion.8
  79.2 1.3 fusion.149
  80.7 0.7 convolution_add_fusion.17
  81.7 0.7 convolution_add_fusion.16
  83.1 0.6 gather_fusion.5
  83.7 0.7 compare_convert_fusion.8
  84.4 1.3 fusion.149
  86.0 0.7 convolution_add_fusion.17
  86.9 0.7 convolution_add_fusion.16
  88.4 0.6 gather_fusion.5
  89.0 0.7 compare_convert_fusion.8
  89.7 1.3 fusion.149
  91.3 0.7 convolution_add_fusion.17
  92.2 0.7 convolution_add_fusion.16
  93.2 10.8 %collective-permute-done.3 = f32[1024,128]{1,0:T(8,128)S(1)} collective-permute-done((f32[1024,128]{1,0:T(8,128)S(1)}, f32[1024,128]{1,0:T(8,128)S(1)}, u32[]{:S(2)}, u32[]{:S(2)}) %collective-permute-start.3) | collective-permute-done | bytes 524320 | tf_op jit(solution)/shard_map/ppermute | solution.py:17
  104.1 1.9 %fusion.48 = f32[1024,128]{1,0:T(8,128)} fusion(f32[1024,128]{1,0:T(8,128)S(1)} %collective-permute-done.3, f32[1024,128]{1,0:T(8,128)} %collective-permute-done.2, f32[8,128,128]{2,1,0:T(8,128)S(1)} %copy.9), kind=kLoop, calls=%fused_computation.89 | loop fusion | flops 262144 | bytes 2097152 | tf_op jit(solution)/shard_map/add | solution.py:99
  106.1 0.8 fusion.44
  106.9 29.7 %all-reduce.2.cloned.1.call-done = f32[1024,128]{1,0:T(8,128)} async-done(((f32[1024,128]{1,0:T(8,128)}), f32[1024,128]{1,0:T(8,128)}) %all-reduce.2.cloned.1.call-update) | async-done | bytes 524304 | tf_op jit(solution)/shard_map/psum | solution.py:100
  136.6 1.8 %fusion.47 = bf16[1024,128]{1,0:T(8,128)(2,1)} fusion(f32[1024,128]{1,0:T(8,128)} %all-reduce.2.cloned.1.call-done, bf16[1024,128]{1,0:T(8,128)(2,1)S(1)} %bitcast.120), kind=kLoop, calls=%fused_computation.87 | loop fusion | flops 786432 | bytes 1048576 | tf_op jit(solution)/shard_map/convert_element_type | solution.py:101
  (82 shorter events, 10.6 us)
Async XLA Ops:
  7.2 129.4 %all-reduce.2.cloned.1.call-start = ((), (), s32[]{:S(2)}) async-start(), calls=%async_computation | async-start | bytes 1048576 | tf_op jit(solution)/shard_map/psum | solution.py:100
  7.2 26.6 %collective-permute-start = (bf16[1024,128]{1,0:T(8,128)(2,1)}, bf16[1024,128]{1,0:T(8,128)(2,1)}, u32[]{:S(2)}, u32[]{:S(2)}) collective-permute-start(bf16[1024,128]{1,0:T(8,128)(2,1)} %param.13), channel_id=1, source_target_pairs={{4,0},{8,4},{12,8},{16,12},{20,16},{24,20},{28,24},{0,28},{5,1},{9... | collective-permute-start | bytes 786440 | tf_op jit(solution)/shard_map/ppermute | solution.py:17
  15.4 4.2 %copy-start.2 = (s32[1,1,3,40]{3,1,2,0:T(1,128)S(1)}, s32[1,1,3,40]{3,1,2,0:T(1,128)}, u32[]{:S(2)}) copy-start(s32[1,1,3,40]{3,1,2,0:T(1,128)} %param.16) | copy-start | bytes 1444
  15.4 4.2 %copy-start.3 = (s32[1,1,3,40]{3,1,2,0:T(1,128)S(1)}, s32[1,1,3,40]{3,1,2,0:T(1,128)}, u32[]{:S(2)}) copy-start(s32[1,1,3,40]{3,1,2,0:T(1,128)} %param.15) | copy-start | bytes 1444
  15.4 4.2 %copy-start = (bf16[1024,128]{1,0:T(8,128)(2,1)S(1)}, bf16[1024,128]{1,0:T(8,128)(2,1)}, u32[]{:S(2)}) copy-start(bf16[1024,128]{1,0:T(8,128)(2,1)} %param.12) | copy-start | bytes 786436
  15.4 4.2 %copy-start.1 = (bf16[1024,128]{1,0:T(8,128)(2,1)S(1)}, bf16[1024,128]{1,0:T(8,128)(2,1)}, u32[]{:S(2)}) copy-start(bf16[1024,128]{1,0:T(8,128)(2,1)} %param.13) | copy-start | bytes 786436
  33.8 32.8 %collective-permute-start.1 = (bf16[1024,128]{1,0:T(8,128)(2,1)}, bf16[1024,128]{1,0:T(8,128)(2,1)S(1)}, u32[]{:S(2)}, u32[]{:S(2)}) collective-permute-start(bf16[1024,128]{1,0:T(8,128)(2,1)} %collective-permute-done), channel_id=1, source_target_pairs={{4,0},{8,4},{12,8},{16,12},{20,16},{24,20},{28,24},{0,28},{5,1},{9... | collective-permute-start | bytes 786440 | tf_op jit(solution)/shard_map/ppermute | solution.py:17
  46.2 47.0 %collective-permute-start.2 = (f32[1024,128]{1,0:T(8,128)S(1)}, f32[1024,128]{1,0:T(8,128)}, u32[]{:S(2)}, u32[]{:S(2)}) collective-permute-start(f32[1024,128]{1,0:T(8,128)S(1)} %bitcast.122), channel_id=1, source_target_pairs={{28,0},{0,4},{4,8},{8,12},{12,16},{16,20},{20,24},{24,28},{29,1},{... | collective-permute-start | bytes 1572872 | tf_op jit(solution)/shard_map/ppermute | solution.py:17
  93.0 11.0 %collective-permute-start.3 = (f32[1024,128]{1,0:T(8,128)S(1)}, f32[1024,128]{1,0:T(8,128)S(1)}, u32[]{:S(2)}, u32[]{:S(2)}) collective-permute-start(f32[1024,128]{1,0:T(8,128)S(1)} %bitcast.123), channel_id=1, source_target_pairs={{24,0},{28,4},{0,8},{4,12},{8,16},{12,20},{16,24},{20,28},{25,1},{... | collective-permute-start | bytes 1572872 | tf_op jit(solution)/shard_map/ppermute | solution.py:17
Sparse Core Ops, SparseCore 0:
  106.1 30.4 all-reduce.1
where the time goes:
time: 143 us; the launch traced here: 145 us
  waiting for transfers between devices  40.5 us (28%)
  matrix products  29.1 us (20%)
  starting transfers between devices  26.6 us (19%)
  local copies, waits for them, and re-layouts  20 us (14%)
  between operations  16.2 us (11%)
  other arithmetic  12.1 us (8%)
    psum x1, waiting for transfers between devices, on_device(): item_sum = lax.psum(item_sum, 'rep')  29.7 us
    ppermute x4, starting transfers between devices, shifted(): return lax.ppermute(block, axis, route)  26.5 us
    ppermute x4, waiting for transfers between devices, shifted(): return lax.ppermute(block, axis, route)  10.9 us
    dot_general x10, matrix products, group_step(): jnp.einsum('gak,gbk->gab', user_rows, item_rows, preferred_element_type=j...  9.84 us
    gather x10, local copies, waits for them, and re-layouts, group_step(): item_rows = item_blocks[item_pick]  7.87 us
    dot_general x10, matrix products, group_step(): jnp.einsum('gn,gak->nak', user_onehot, user_terms, precision=lax.Precisio...  7.14 us
    dot_general x10, matrix products, group_step(): jnp.einsum('gn,gak->nak', item_onehot, item_terms, precision=lax.Precisio...  7.13 us
    convert_element_type x10, other arithmetic, group_step(): valid_slots = (first_slot + group_slots < live_count).astype(jnp.float32)  6.57 us
  transfers between devices with their start and end apart: 5, of which 2 were waited for; matrix products, arithmetic and copies ran while one was open for 39% of the time, Pallas kernels for 0%

commit v1 on v0

v1 whole, which is shorter than its diff:
```python
import functools
import math

import jax
import jax.numpy as jnp
from jax import lax
from jax.experimental import pallas as pl
from jax.experimental.pallas import tpu as pltpu
from jax.sharding import PartitionSpec as P

confidence = 0.5
shrinkage = 0.05
step_gain = 0.3
group = 8
cores = 2

NT = (((1,), (1,)), ((), ()))
NN = (((1,), (0,)), ((), ()))


def mul(a, b, dims):
    return lax.dot_general(a, b, dims, preferred_element_type=jnp.float32)


def tile_rows(index, tile):
    return pl.ds(pl.multiple_of(index * tile, tile), tile)


def stop_kernel(which, first, last, rate, *refs):
    if first:
        counts, user_tiles, item_tiles, users, items, ratings = refs[:6]
        refs = refs[6:]
    else:
        counts, user_tiles, item_tiles, users, items, ratings, grad_in = refs[:7]
        refs = refs[7:]
    user_out, item_out, counts_s, ut_s, it_s, users_v, items_v, rbuf, users_t, total, item_t = refs[:11]
    small, arrive = refs[11:]
    tile = ratings.shape[-1]
    slots = ratings.shape[3]
    n_user = users.shape[0] // tile
    n_item = items.shape[0] // tile
    stop = which(lax.rem(lax.axis_index("rep"), cores))
    copies = [
        pltpu.make_async_copy(counts.at[0, 0], counts_s, small.at[0]),
        pltpu.make_async_copy(user_tiles.at[0], ut_s, small.at[1]),
        pltpu.make_async_copy(item_tiles.at[0], it_s, small.at[2]),
        pltpu.make_async_copy(users, users_v, small.at[3]),
        pltpu.make_async_copy(items, items_v, small.at[4]),
    ]
    if not first:
        copies.append(pltpu.make_async_copy(grad_in, total, small.at[5]))
    for copy in copies:
        copy.start()
    copies[0].wait()
    live = counts_s[stop]
    groups = lax.div(live + group - 1, group)

    def tiles_copy(g):
        rows = pl.ds(g * group, group)
        return pltpu.make_async_copy(ratings.at[0, 0, stop, rows], rbuf.at[rows], arrive.at[g])

    def start_copy(g, carry):
        tiles_copy(g).start()
        return carry

    lax.fori_loop(0, groups, start_copy, 0)
    item_t[...] = jnp.zeros_like(item_t)
    if first:
        total[...] = jnp.zeros_like(total)
    for copy in copies[1:]:
        copy.wait()
    for t in range(n_user):
        users_t[t] = users_v[pl.ds(t * tile, tile)].T

    def step(g, carry):
        tiles_copy(g).wait()
        slots_now = []
        for k in range(group):
            s = g * group + k
            u_index = ut_s[stop, 0, s]
            i_index = it_s[stop, 0, s]
            u = users_v[tile_rows(u_index, tile)]
            v = items_v[tile_rows(i_index, tile)]
            r = rbuf[s].astype(jnp.float32)
            e = (1.0 + confidence * r) * (r - mul(u, v, NT))
            e = jnp.where(s < live, e, 0.0).astype(jnp.bfloat16)
            slots_now.append((u_index, i_index, v, e))
        terms = [(a, b, mul(e, v, NN), mul(users_t[a], e, NN)) for a, b, v, e in slots_now]
        for a, b, to_user, to_item in terms:
            total[tile_rows(a, tile)] += to_user
            item_t[b] += to_item
        return carry

    lax.fori_loop(0, groups, step, 0)
    for t in range(n_item):
        item_out[pl.ds(t * tile, tile)] = item_t[t].T
    if last:
        u32 = users_v[...].astype(jnp.float32)
        user_out[...] = (u32 - rate * (total[...] + shrinkage * u32)).astype(user_out.dtype)
    else:
        user_out[...] = total[...]


def meet(which, arrays, grad_in=None, last=False, rate=0.0):
    counts, user_tiles, item_tiles, users, items, ratings = arrays
    first = grad_in is None
    tile, slots, stops = ratings.shape[-1], ratings.shape[3], ratings.shape[2]
    rank = users.shape[1]
    anywhere = pl.BlockSpec(memory_space=pltpu.HBM)
    vmem = pl.BlockSpec(memory_space=pltpu.VMEM)
    operands = list(arrays) + ([] if first else [grad_in])
    return pl.pallas_call(
        functools.partial(stop_kernel, which, first, last, rate),
        out_shape=(
            jax.ShapeDtypeStruct(users.shape, users.dtype if last else jnp.float32),
            jax.ShapeDtypeStruct(items.shape, jnp.float32),
        ),
        in_specs=[anywhere] * len(operands),
        out_specs=(vmem, vmem),
        scratch_shapes=[
            pltpu.SMEM((stops,), jnp.int32),
            pltpu.SMEM((stops, 1, slots), jnp.int32),
            pltpu.SMEM((stops, 1, slots), jnp.int32),
            pltpu.VMEM(users.shape, users.dtype),
            pltpu.VMEM(items.shape, items.dtype),
            pltpu.VMEM((slots, tile, tile), ratings.dtype),
            pltpu.VMEM((users.shape[0] // tile, rank, tile), users.dtype),
            pltpu.VMEM(users.shape, jnp.float32),
            pltpu.VMEM((items.shape[0] // tile, rank, tile), jnp.float32),
            pltpu.SemaphoreType.DMA((6,)),
            pltpu.SemaphoreType.DMA((slots // group,)),
        ],
        compiler_params=pltpu.CompilerParams(vmem_limit_bytes=16 * 2**20),
        cost_estimate=pl.CostEstimate(flops=10**10, bytes_accessed=8 * 10**6, transcendentals=0),
    )(*operands)


def joint(block, target):
    n_blk, n_rep = lax.axis_size("blk"), lax.axis_size("rep")
    route = []
    for b in range(n_blk):
        for r in range(n_rep):
            to_b, to_r = target(b, r)
            route.append((b * n_rep + r, (to_b % n_blk) * n_rep + to_r))
    return lax.ppermute(block, ("blk", "rep"), route)


def swap(block, bit):
    return lax.ppermute(block, "rep", [(r, r ^ bit) for r in range(lax.axis_size("rep"))])


def on_device(users, items, ratings, user_tiles, item_tiles, counts):
    tile, slots, stops = ratings.shape[-1], ratings.shape[3], ratings.shape[2]
    n_rep = lax.axis_size("rep")
    core = lax.rem(lax.axis_index("rep"), cores)
    slot_cells = stops * slots * tile * tile
    rate_user = step_gain / math.sqrt(slot_cells / users.shape[0])
    rate_item = step_gain / math.sqrt(n_rep * slot_cells / items.shape[0])
    bound = cores * slots * tile * 2.0 * 3.0 * (4.0 + 4.0 * users.shape[1])
    scale = 2.0 ** math.floor(math.log2(60000.0 / bound))

    user_tiles, item_tiles = (a.transpose(0, 2, 1, 3) for a in (user_tiles, item_tiles))

    fixed = [pltpu.with_memory_space_constraint(a, pltpu.HBM) for a in (counts, user_tiles, item_tiles, users, ratings)]

    def arrays(block):
        return (*fixed[:4], block, fixed[4])

    near = joint(items, lambda b, r: (b - 2 + r % cores, r))
    grad_user, own = meet(lambda c: c * 0, arrays(pltpu.with_memory_space_constraint(items, pltpu.HBM)))
    far = swap(near, 1)
    grad_user, given = meet(lambda c: 2 - c, arrays(near), grad_user)
    taken = swap(given, 1)
    user_new, kept = meet(lambda c: 1 + c, arrays(far), grad_user, True, rate_user)
    sent = ((kept + taken) * scale).astype(jnp.float16)
    come = joint(sent, lambda b, r: (b + 1 + r % cores, r)).astype(jnp.float32) * (1.0 / scale)
    column = come + own
    half = items.shape[0] // cores
    mine = lax.dynamic_slice_in_dim(column, core * half, half)
    theirs = lax.dynamic_slice_in_dim(column, (1 - core) * half, half)
    chip = mine + swap(theirs, 1)
    bit = cores
    while bit < n_rep:
        coded = lax.optimization_barrier((chip * scale).astype(jnp.float16))
        both = coded.astype(jnp.float32) + swap(coded, bit).astype(jnp.float32)
        chip = both * (1.0 / scale)
        bit *= 2
    items32 = lax.dynamic_slice_in_dim(items, core * half, half).astype(jnp.float32)
    new_half = (items32 - rate_item * (chip + shrinkage * items32)).astype(items.dtype)
    other_half = swap(new_half, 1)
    low = jnp.where(core == 0, new_half, other_half)
    high = jnp.where(core == 0, other_half, new_half)
    return user_new, jnp.concatenate([low, high])


def solution(mesh):
    return jax.shard_map(
        on_device,
        mesh=mesh,
        in_specs=(
            P(("blk", "rep"), None),
            P("blk", None),
            P("blk", "rep", None, None, None, None),
            P("blk", "rep", None, None),
            P("blk", "rep", None, None),
            P("blk", "rep", None),
        ),
        out_specs=(P(("blk", "rep"), None), P("blk", None)),
        check_vma=False,
    )
```

time: 143 us -> 41.6 us (0.29); the launches traced: 145 us -> 41.3 us
  matrix products: 29.1 us -> 0 us
  local copies, waits for them, and re-layouts: 20 us -> 0.03 us
  starting transfers between devices: 26.6 us -> 7.01 us
  waiting for transfers between devices: 40.5 us -> 21.9 us
  between operations: 16.2 us -> 0.74 us
  other arithmetic: 12.1 us -> 1.01 us
  Pallas kernels: 0 us -> 10.6 us
    psum x1 -> x0, waiting for transfers between devices: 29.7 us -> none  [on_device(): item_sum = lax.psum(item_sum, 'rep')]
    dot_general x50 -> x0, matrix products: 29.1 us -> none  [the longest x10 9.84 us: group_step(): jnp.einsum('gak,gbk->gab', user_rows, item_rows, preferred_element_type=j...]
    ppermute x4 -> x7, starting transfers between devices: 26.5 us -> 7.01 us  [the longest x2 5.16 us: joint(): return lax.ppermute(block, ('blk', 'rep'), route)]
    gather x20 -> x0, local copies, waits for them, and re-layouts: 13.8 us -> none  [the longest x10 7.87 us: group_step(): item_rows = item_blocks[item_pick]]
    ppermute x4 -> x7, waiting for transfers between devices: 10.9 us -> 21.9 us  [the longest x2 14.6 us: joint(): return lax.ppermute(block, ('blk', 'rep'), route)]
    pallas_call x0 -> x3, Pallas kernels: none -> 10.6 us  [meet(): pl.pallas_call(functools.partial(stop_kernel, which, first, last, rate),...]
    convert_element_type x12 -> x3, other arithmetic: 9.23 us -> 0.21 us  [the longest x1 0.1 us: on_device(): (items32 - rate_item * (chip + shrinkage * items32)).astype(items.dtype)]
    squeeze x2 -> x0, local copies, waits for them, and re-layouts: 4.12 us -> none  [the longest x1 4.12 us: on_device(): stop_ratings = ratings[0, 0, station]]
  transfers between devices with their start and end apart: 5 -> 7, of which waited for: 2 -> 5; matrix products, arithmetic and copies ran while one was open for 39% -> 0% of each run, Pallas kernels for 0% -> 26%
where the time goes in v1:
time: 41.6 us; the launch traced here: 41.3 us
  waiting for transfers between devices  21.9 us (53%)
  Pallas kernels  10.6 us (25%)
  starting transfers between devices  7.01 us (17%)
  other arithmetic  1.01 us (2%)
  between operations  0.74 us (2%)
    ppermute x2, waiting for transfers between devices, joint(): return lax.ppermute(block, ('blk', 'rep'), route)  14.6 us
    pallas_call x3, Pallas kernels, meet(): pl.pallas_call(functools.partial(stop_kernel, which, first, last, rate),...  10.6 us
    ppermute x5, waiting for transfers between devices, swap(): lax.ppermute(block, 'rep', [(r, r ^ bit) for r in range(lax.axis_size('re...  7.34 us
    ppermute x2, starting transfers between devices, joint(): return lax.ppermute(block, ('blk', 'rep'), route)  5.16 us
    ppermute x5, starting transfers between devices, swap(): lax.ppermute(block, 'rep', [(r, r ^ bit) for r in range(lax.axis_size('re...  1.85 us
  transfers between devices with their start and end apart: 7, of which 5 were waited for; matrix products, arithmetic and copies ran while one was open for 0% of the time, Pallas kernels for 26%

profile of v1, /device:TPU:0, one launch (start us, length us, event | category | flops | bytes accessed | tf_op | source)
XLA Modules:
  0.0 41.3 jit_solution(7940344310407778712)
XLA Ops:
  0.6 5.1 %collective-permute-start = (bf16[1024,128]{1,0:T(8,128)(2,1)}, bf16[1024,128]{1,0:T(8,128)(2,1)S(1)}, u32[]{:S(2)}, u32[]{:S(2)}) collective-permute-start(bf16[1024,128]{1,0:T(8,128)(2,1)} %refs_4_.1), channel_id=1, source_target_pairs={{0,24},{1,29},{2,26},{3,31},{4,28},{5,1},{6,30},{7,3},{8,0},{9,5},... | collective-permute-start | bytes 786440 | tf_op jit(solution)/shard_map/ppermute | solution.py:145
  5.7 2.9 %shard_map.77 = (f32[1024,128]{1,0:T(8,128)S(1)}, f32[1024,128]{1,0:T(8,128)S(1)}) custom-call(s32[1,1,3]{2,1,0:T(1,128)} %refs_0_.5, s32[1,3,1,40]{3,2,1,0:T(1,128)} %bitcast.2, s32[1,3,1,40]{3,2,1,0:T(1,128)} %bitcast.5, bf16[1024,128]{1,0:T(8,128)(2,1)} %refs_3_.5, bf16[1024,128]{1,0:T(8,128)(2,1)} %refs_4_.1, bf16[1,1,3,40,128,128]{5,4,3,2,1,0:T(8,128)(2,1)} %refs_5_.5), custom_call_target="tpu_custom_call" | custom-call | flops 10000000000 | bytes 8000000 | tf_op jit(solution)/shard_map/pallas_call | solution.py:112
  8.6 3.9 %collective-permute-done.refs_4_ = bf16[1024,128]{1,0:T(8,128)(2,1)S(1)} collective-permute-done((bf16[1024,128]{1,0:T(8,128)(2,1)}, bf16[1024,128]{1,0:T(8,128)(2,1)S(1)}, u32[]{:S(2)}, u32[]{:S(2)}) %collective-permute-start) | collective-permute-done | bytes 262176 | tf_op jit(solution)/shard_map/ppermute | solution.py:145
  12.6 0.0 collective-permute-start.1
  12.6 4.3 %shard_map.78 = (f32[1024,128]{1,0:T(8,128)S(1)}, f32[1024,128]{1,0:T(8,128)S(1)}) custom-call(s32[1,1,3]{2,1,0:T(1,128)} %refs_0_.5, s32[1,3,1,40]{3,2,1,0:T(1,128)} %bitcast.3, s32[1,3,1,40]{3,2,1,0:T(1,128)} %bitcast.6, bf16[1024,128]{1,0:T(8,128)(2,1)} %refs_3_.5, bf16[1024,128]{1,0:T(8,128)(2,1)S(1)} %collective-permute-done.refs_4_, ...), custom_call_target="tpu_custom_call" | custom-call | flops 10000000000 | bytes 8000000 | tf_op jit(solution)/shard_map/pallas_call | solution.py:112
  16.9 0.6 %collective-permute-start.2 = (f32[1024,128]{1,0:T(8,128)S(1)}, f32[1024,128]{1,0:T(8,128)S(1)}, u32[]{:S(2)}, u32[]{:S(2)}) collective-permute-start(f32[1024,128]{1,0:T(8,128)S(1)} %get-tuple-element.12), channel_id=1, source_target_pairs={{0,1},{1,0},{2,3},{3,2},{4,5},{5,4},{6,7},{7,6},{8,9},{9,8},{10,11... | collective-permute-start | bytes 1572872 | tf_op jit(solution)/shard_map/ppermute | solution.py:149
  17.5 0.0 collective-permute-done.1.refs_4_
  17.5 0.0 copy-start
  17.5 3.4 %shard_map.79 = (bf16[1024,128]{1,0:T(8,128)(2,1)}, f32[1024,128]{1,0:T(8,128)S(1)}) custom-call(s32[1,1,3]{2,1,0:T(1,128)} %refs_0_.5, s32[1,3,1,40]{3,2,1,0:T(1,128)} %bitcast.4, s32[1,3,1,40]{3,2,1,0:T(1,128)} %bitcast.7, bf16[1024,128]{1,0:T(8,128)(2,1)} %refs_3_.5, bf16[1024,128]{1,0:T(8,128)(2,1)S(1)} %collective-permute-done.1.refs_4_, ...), custom_call_target="tpu_custom_call" | custom-call | flops 10000000000 | bytes 8000000 | tf_op jit(solution)/shard_map/pallas_call | solution.py:112
  20.8 0.0 collective-permute-done.2
  20.9 0.1 multiply_convert_fusion
  20.9 0.1 collective-permute-start.3
  21.0 10.7 %collective-permute-done.3 = f16[1024,128]{1,0:T(8,128)(2,1)S(1)} collective-permute-done((f16[1024,128]{1,0:T(8,128)(2,1)S(1)}, f16[1024,128]{1,0:T(8,128)(2,1)S(1)}, u32[]{:S(2)}, u32[]{:S(2)}) %collective-permute-start.3) | collective-permute-done | bytes 262176 | tf_op jit(solution)/shard_map/ppermute | solution.py:145
  31.7 0.1 multiply_add_fusion
  31.8 0.1 collective-permute-start.4
  31.9 1.5 %collective-permute-done.4 = f32[512,128]{1,0:T(8,128)S(1)} collective-permute-done((f32[512,128]{1,0:T(8,128)S(1)}, f32[512,128]{1,0:T(8,128)S(1)}, u32[]{:S(2)}, u32[]{:S(2)}) %collective-permute-start.4) | collective-permute-done | bytes 262176 | tf_op jit(solution)/shard_map/ppermute | solution.py:149
  33.4 1.1 %collective-permute-start.5 = (f16[512,128]{1,0:T(8,128)(2,1)S(1)}, f16[512,128]{1,0:T(8,128)(2,1)S(1)}, u32[]{:S(2)}, u32[]{:S(2)}) collective-permute-start(f16[512,128]{1,0:T(8,128)(2,1)S(1)} %multiply_convert_fusion.1), channel_id=1, source_target_pairs={{0,2},{1,3},{2,0},{3,1},{4,6},{5,7},{6,4},{7,5},{8,10},{9,11},{10,... | collective-permute-start | bytes 393224 | tf_op jit(solution)/shard_map/ppermute | solution.py:149
  34.5 4.5 %collective-permute-done.5 = f16[512,128]{1,0:T(8,128)(2,1)S(1)} collective-permute-done((f16[512,128]{1,0:T(8,128)(2,1)S(1)}, f16[512,128]{1,0:T(8,128)(2,1)S(1)}, u32[]{:S(2)}, u32[]{:S(2)}) %collective-permute-start.5) | collective-permute-done | bytes 131104 | tf_op jit(solution)/shard_map/ppermute | solution.py:149
  39.0 0.0 copy-done
  39.0 0.1 fusion.2
  39.1 0.1 collective-permute-start.6
  39.2 1.3 %collective-permute-done.6 = bf16[512,128]{1,0:T(8,128)(2,1)S(1)} collective-permute-done((bf16[512,128]{1,0:T(8,128)(2,1)S(1)}, bf16[512,128]{1,0:T(8,128)(2,1)S(1)}, u32[]{:S(2)}, u32[]{:S(2)}) %collective-permute-start.6) | collective-permute-done | bytes 131104 | tf_op jit(solution)/shard_map/ppermute | solution.py:149
  40.6 0.7 %pad_maximum_fusion = bf16[1024,128]{1,0:T(8,128)(2,1)} fusion(bf16[512,128]{1,0:T(8,128)(2,1)S(1)} %get-tuple-element.15, bf16[512,128]{1,0:T(8,128)(2,1)S(1)} %get-tuple-element.14), kind=kLoop, calls=%fused_computation.7 | loop fusion | flops 524288 | bytes 524288 | tf_op jit(solution)/shard_map/concatenate | solution.py:193
  (3 shorter events, 0.1 us)
Async XLA Ops:
  0.6 11.9 %collective-permute-start = (bf16[1024,128]{1,0:T(8,128)(2,1)}, bf16[1024,128]{1,0:T(8,128)(2,1)S(1)}, u32[]{:S(2)}, u32[]{:S(2)}) collective-permute-start(bf16[1024,128]{1,0:T(8,128)(2,1)} %refs_4_.1), channel_id=1, source_target_pairs={{0,24},{1,29},{2,26},{3,31},{4,28},{5,1},{6,30},{7,3},{8,0},{9,5},... | collective-permute-start | bytes 786440 | tf_op jit(solution)/shard_map/ppermute | solution.py:145
  12.6 4.9 %collective-permute-start.1 = (bf16[1024,128]{1,0:T(8,128)(2,1)S(1)}, bf16[1024,128]{1,0:T(8,128)(2,1)S(1)}, u32[]{:S(2)}, u32[]{:S(2)}) collective-permute-start(bf16[1024,128]{1,0:T(8,128)(2,1)S(1)} %collective-permute-done.refs_4_), channel_id=1, source_target_pairs={{0,1},{1,0},{2,3},{3,2},{4,5},{5,4},{6,7},{7,6},{8,9},{9,8},{10,11... | collective-permute-start | bytes 786440 | tf_op jit(solution)/shard_map/ppermute | solution.py:149
  16.9 4.0 %collective-permute-start.2 = (f32[1024,128]{1,0:T(8,128)S(1)}, f32[1024,128]{1,0:T(8,128)S(1)}, u32[]{:S(2)}, u32[]{:S(2)}) collective-permute-start(f32[1024,128]{1,0:T(8,128)S(1)} %get-tuple-element.12), channel_id=1, source_target_pairs={{0,1},{1,0},{2,3},{3,2},{4,5},{5,4},{6,7},{7,6},{8,9},{9,8},{10,11... | collective-permute-start | bytes 1572872 | tf_op jit(solution)/shard_map/ppermute | solution.py:149
  17.5 21.6 %copy-start = (bf16[1024,128]{1,0:T(8,128)(2,1)S(1)}, bf16[1024,128]{1,0:T(8,128)(2,1)}, u32[]{:S(2)}) copy-start(bf16[1024,128]{1,0:T(8,128)(2,1)} %refs_4_.1) | copy-start | bytes 786436
  20.9 10.8 %collective-permute-start.3 = (f16[1024,128]{1,0:T(8,128)(2,1)S(1)}, f16[1024,128]{1,0:T(8,128)(2,1)S(1)}, u32[]{:S(2)}, u32[]{:S(2)}) collective-permute-start(f16[1024,128]{1,0:T(8,128)(2,1)S(1)} %multiply_convert_fusion), channel_id=1, source_target_pairs={{0,4},{1,9},{2,6},{3,11},{4,8},{5,13},{6,10},{7,15},{8,12},{9,17},... | collective-permute-start | bytes 786440 | tf_op jit(solution)/shard_map/ppermute | solution.py:145
  31.8 1.6 %collective-permute-start.4 = (f32[512,128]{1,0:T(8,128)S(1)}, f32[512,128]{1,0:T(8,128)S(1)}, u32[]{:S(2)}, u32[]{:S(2)}) collective-permute-start(f32[512,128]{1,0:T(8,128)S(1)} %constant_dynamic-slice_fusion), channel_id=1, source_target_pairs={{0,1},{1,0},{2,3},{3,2},{4,5},{5,4},{6,7},{7,6},{8,9},{9,8},{10,11... | collective-permute-start | bytes 786440 | tf_op jit(solution)/shard_map/ppermute | solution.py:149
  33.4 5.6 %collective-permute-start.5 = (f16[512,128]{1,0:T(8,128)(2,1)S(1)}, f16[512,128]{1,0:T(8,128)(2,1)S(1)}, u32[]{:S(2)}, u32[]{:S(2)}) collective-permute-start(f16[512,128]{1,0:T(8,128)(2,1)S(1)} %multiply_convert_fusion.1), channel_id=1, source_target_pairs={{0,2},{1,3},{2,0},{3,1},{4,6},{5,7},{6,4},{7,5},{8,10},{9,11},{10,... | collective-permute-start | bytes 393224 | tf_op jit(solution)/shard_map/ppermute | solution.py:149
  39.1 1.4 %collective-permute-start.6 = (bf16[512,128]{1,0:T(8,128)(2,1)S(1)}, bf16[512,128]{1,0:T(8,128)(2,1)S(1)}, u32[]{:S(2)}, u32[]{:S(2)}) collective-permute-start(bf16[512,128]{1,0:T(8,128)(2,1)S(1)} %fusion.2), channel_id=1, source_target_pairs={{0,1},{1,0},{2,3},{3,2},{4,5},{5,4},{6,7},{7,6},{8,9},{9,8},{10,11... | collective-permute-start | bytes 393224 | tf_op jit(solution)/shard_map/ppermute | solution.py:149

commit v2 on v1

v2 whole, which is shorter than its diff:
```python
import functools
import math

import jax
import jax.numpy as jnp
from jax import lax
from jax.experimental import pallas as pl
from jax.experimental.pallas import tpu as pltpu
from jax.sharding import PartitionSpec as P

confidence = 0.5
shrinkage = 0.05
step_gain = 0.3
chunk = 8
group = 8
cores = 2
f32, bf16, f16 = jnp.float32, jnp.bfloat16, jnp.float16

NT = (((1,), (1,)), ((), ()))
NN = (((1,), (0,)), ((), ()))
anywhere = pl.BlockSpec(memory_space=pl.ANY)
vmem = pl.BlockSpec(memory_space=pltpu.VMEM)


def mul(a, b, dims):
    return lax.dot_general(a, b, dims, preferred_element_type=f32)


def tile_rows(index, tile):
    return pl.ds(pl.multiple_of(index * tile, tile), tile)


def near_stop(core):
    return 2 - core


def far_stop(core):
    return 1 + core


def steps(live, size):
    return lax.div(live + size - 1, size)


def run_slots(live, stop, ut_s, it_s, users, users_t, block, tiles, total, item_t):
    tile = tiles.shape[-1]

    def step(g, carry):
        slots_now = []
        for k in range(group):
            s = g * group + k
            listed = jnp.minimum(s, ut_s.shape[-1] - 1)
            u_index = ut_s[stop, 0, listed]
            i_index = it_s[stop, 0, listed]
            u = users[tile_rows(u_index, tile)]
            v = block[tile_rows(i_index, tile)]
            r = tiles[s].astype(f32)
            e = (1.0 + confidence * r) * (r - mul(u, v, NT))
            e = jnp.where(s < live, e, 0.0).astype(bf16)
            slots_now.append((u_index, i_index, v, e))
        terms = [(a, b, mul(e, v, NN), mul(users_t[a], e, NN)) for a, b, v, e in slots_now]
        for a, b, to_user, to_item in terms:
            total[tile_rows(a, tile)] += to_user
            item_t[b] += to_item
        return carry

    lax.fori_loop(0, steps(live, group), step, 0)


class Tiles:
    def __init__(self, ratings, stop, counts, place, sems):
        self.ratings, self.stop, self.place, self.sems = ratings, stop, place, sems
        self.count = steps(counts[stop], chunk)

    def copy(self, g):
        rows = pl.ds(g * chunk, chunk)
        return pltpu.make_async_copy(self.ratings.at[0, 0, self.stop, rows], self.place.at[rows], self.sems.at[g])

    def start(self):
        def begin(g, carry):
            self.copy(g).start()
            return carry

        lax.fori_loop(0, self.count, begin, 0)

    def wait(self):
        def finish(g, carry):
            self.copy(g).wait()
            return carry

        lax.fori_loop(0, self.count, finish, 0)


def own_kernel(
    counts, user_tiles, item_tiles, users, items, ratings,
    total, own_t, near_r, users_v, users_t, counts_v, ut_v, it_v,
    counts_s, ut_s, it_s, items_v, own_r, small, arrive,
):
    tile = ratings.shape[-1]
    core = lax.rem(lax.axis_index("rep"), cores)
    lists = [
        pltpu.make_async_copy(counts.at[0, 0], counts_s, small.at[0]),
        pltpu.make_async_copy(user_tiles.at[0], ut_s, small.at[1]),
        pltpu.make_async_copy(item_tiles.at[0], it_s, small.at[2]),
    ]
    blocks = [
        pltpu.make_async_copy(users, users_v, small.at[3]),
        pltpu.make_async_copy(items, items_v, small.at[4]),
        pltpu.make_async_copy(counts, counts_v, small.at[5]),
        pltpu.make_async_copy(user_tiles, ut_v, small.at[6]),
        pltpu.make_async_copy(item_tiles, it_v, small.at[7]),
    ]
    for copy in lists + blocks:
        copy.start()
    lists[0].wait()
    plans = [
        Tiles(ratings, 0, counts_s, own_r, arrive.at[0]),
        Tiles(ratings, near_stop(core), counts_s, near_r, arrive.at[1]),
    ]
    for plan in plans:
        plan.start()
    total[...] = jnp.zeros_like(total)
    own_t[...] = jnp.zeros_like(own_t)
    for copy in lists[1:] + blocks:
        copy.wait()
    for t in range(users_t.shape[0]):
        users_t[t] = users_v[pl.ds(t * tile, tile)].T
    plans[0].wait()
    run_slots(counts_s[0], 0, ut_s, it_s, users_v, users_t, items_v, own_r, total, own_t)
    plans[1].wait()


def own_call(counts, user_tiles, item_tiles, users, items, ratings):
    tile, slots, stops, rank = ratings.shape[-1], ratings.shape[3], ratings.shape[2], users.shape[1]
    n_user, n_item = users.shape[0] // tile, items.shape[0] // tile
    some_tiles = (-(-slots // group) * group, tile, tile)
    shape = jax.ShapeDtypeStruct
    return pl.pallas_call(
        own_kernel,
        out_shape=(
            shape(users.shape, f32),
            shape((n_item, rank, tile), f32),
            shape(some_tiles, ratings.dtype),
            shape(users.shape, users.dtype),
            shape((n_user, rank, tile), users.dtype),
            shape(counts.shape, counts.dtype),
            shape(user_tiles.shape, user_tiles.dtype),
            shape(item_tiles.shape, item_tiles.dtype),
        ),
        in_specs=[anywhere] * 6,
        out_specs=[vmem] * 8,
        scratch_shapes=[
            pltpu.SMEM((stops,), jnp.int32),
            pltpu.SMEM((stops, 1, slots), jnp.int32),
            pltpu.SMEM((stops, 1, slots), jnp.int32),
            pltpu.VMEM(items.shape, items.dtype),
            pltpu.VMEM(some_tiles, ratings.dtype),
            pltpu.SemaphoreType.DMA((8,)),
            pltpu.SemaphoreType.DMA((2, slots // chunk)),
        ],
        compiler_params=pltpu.CompilerParams(vmem_limit_bytes=8 * 2**20),
        cost_estimate=pl.CostEstimate(flops=10**10, bytes_accessed=8 * 10**6, transcendentals=0),
    )(*[pltpu.with_memory_space_constraint(a, pltpu.HBM) for a in (counts, user_tiles, item_tiles, users, items, ratings)])


def stop_kernel(which, following, *refs):
    counts_v, ut_v, it_v, users, users_t, block, tiles = refs[:7]
    refs = refs[8:]
    if following is not None:
        ratings, total, item_t, tiles_next, counts_s, ut_s, it_s, small, arrive = refs
    else:
        total, item_t, counts_s, ut_s, it_s, small = refs
    lists = [
        pltpu.make_async_copy(counts_v.at[0, 0], counts_s, small.at[0]),
        pltpu.make_async_copy(ut_v.at[0], ut_s, small.at[1]),
        pltpu.make_async_copy(it_v.at[0], it_s, small.at[2]),
    ]
    for copy in lists:
        copy.start()
    item_t[...] = jnp.zeros_like(item_t)
    for copy in lists:
        copy.wait()
    core = lax.rem(lax.axis_index("rep"), cores)
    if following is not None:
        plan = Tiles(ratings, following(core), counts_s, tiles_next, arrive)
        plan.start()
    stop = which(core)
    run_slots(counts_s[stop], stop, ut_s, it_s, users, users_t, block, tiles, total, item_t)
    if following is not None:
        plan.wait()


def stop_call(which, lists, users, users_t, block, tiles, total, following=None, ratings=None):
    slots, tile = lists[1].shape[-1], tiles.shape[-1]
    stops = lists[0].shape[-1]
    operands = [*lists, users, users_t, block, tiles, total]
    out_shape = [
        jax.ShapeDtypeStruct(total.shape, f32),
        jax.ShapeDtypeStruct((block.shape[0] // tile, block.shape[1], tile), f32),
    ]
    scratch = [
        pltpu.SMEM((stops,), jnp.int32),
        pltpu.SMEM((stops, 1, slots), jnp.int32),
        pltpu.SMEM((stops, 1, slots), jnp.int32),
        pltpu.SemaphoreType.DMA((3,)),
    ]
    in_specs = [vmem] * len(operands)
    aliases = {len(operands) - 1: 0}
    if following is not None:
        operands.append(pltpu.with_memory_space_constraint(ratings, pltpu.HBM))
        in_specs.append(anywhere)
        out_shape.append(jax.ShapeDtypeStruct(tiles.shape, tiles.dtype))
        scratch.append(pltpu.SemaphoreType.DMA((slots // chunk,)))
    return pl.pallas_call(
        functools.partial(stop_kernel, which, following),
        out_shape=out_shape,
        in_specs=in_specs,
        out_specs=[vmem] * len(out_shape),
        input_output_aliases=aliases,
        scratch_shapes=scratch,
        compiler_params=pltpu.CompilerParams(vmem_limit_bytes=4 * 2**20),
        cost_estimate=pl.CostEstimate(flops=10**10, bytes_accessed=8 * 10**6, transcendentals=0),
    )(*operands)


def joint(block, target):
    n_blk, n_rep = lax.axis_size("blk"), lax.axis_size("rep")
    route = []
    for b in range(n_blk):
        for r in range(n_rep):
            to_b, to_r = target(b, r)
            route.append((b * n_rep + r, (to_b % n_blk) * n_rep + to_r))
    return lax.ppermute(block, ("blk", "rep"), route)


def swap(block, bit):
    return lax.ppermute(block, "rep", [(r, r ^ bit) for r in range(lax.axis_size("rep"))])


def on_device(users, items, ratings, user_tiles, item_tiles, counts):
    tile, slots, stops = ratings.shape[-1], ratings.shape[3], ratings.shape[2]
    n_rep = lax.axis_size("rep")
    core = lax.rem(lax.axis_index("rep"), cores)
    slot_cells = stops * slots * tile * tile
    rate_user = step_gain / math.sqrt(slot_cells / users.shape[0])
    rate_item = step_gain / math.sqrt(n_rep * slot_cells / items.shape[0])
    bound = cores * slots * tile * 2.0 * 3.0 * (4.0 + 4.0 * users.shape[1])
    scale = 2.0 ** math.floor(math.log2(60000.0 / bound))

    near = joint(items, lambda b, r: (b - near_stop(r % cores), r))
    user_tiles, item_tiles = (a.transpose(0, 2, 1, 3) for a in (user_tiles, item_tiles))
    total, own, near_r, users_v, users_t, *lists = own_call(
        counts, user_tiles, item_tiles, users, items, ratings
    )
    far = swap(near, 1)
    total, given, far_r = stop_call(near_stop, lists, users_v, users_t, near, near_r, total, far_stop, ratings)
    taken = swap(given, 1)
    total, kept = stop_call(far_stop, lists, users_v, users_t, far, far_r, total)
    users32 = users_v.astype(f32)
    user_new = (users32 - rate_user * (total + shrinkage * users32)).astype(users.dtype)
    both = kept + taken
    half = both.shape[0] // cores

    def half_of(array, c):
        return lax.dynamic_slice_in_dim(array, c * half, half)

    straight = joint((half_of(both, core) * scale).astype(f16), lambda b, r: (b + far_stop(r % cores), r))
    across = joint((half_of(both, 1 - core) * scale).astype(f16), lambda b, r: (b + far_stop(r % cores), r ^ 1))
    own_half = half_of(own, core) + swap(half_of(own, 1 - core), 1)
    chip = own_half + (straight.astype(f32) + across.astype(f32)) * (1.0 / scale)
    bit = cores
    while bit < n_rep:
        coded = lax.optimization_barrier((chip * scale).astype(f16))
        chip = (coded.astype(f32) + swap(coded, bit).astype(f32)) * (1.0 / scale)
        bit *= 2
    chip = chip.transpose(0, 2, 1).reshape(-1, users.shape[1])
    rows = items.shape[0] // cores
    items32 = lax.dynamic_slice_in_dim(items, core * rows, rows).astype(f32)
    new_half = (items32 - rate_item * (chip + shrinkage * items32)).astype(items.dtype)
    other_half = swap(new_half, 1)
    low = jnp.where(core == 0, new_half, other_half)
    high = jnp.where(core == 0, other_half, new_half)
    return user_new, jnp.concatenate([low, high])


def solution(mesh):
    return jax.shard_map(
        on_device,
        mesh=mesh,
        in_specs=(
            P(("blk", "rep"), None),
            P("blk", None),
            P("blk", "rep", None, None, None, None),
            P("blk", "rep", None, None),
            P("blk", "rep", None, None),
            P("blk", "rep", None),
        ),
        out_specs=(P(("blk", "rep"), None), P("blk", None)),
        check_vma=False,
    )
```

time: 41.6 us -> 34.9 us (0.84)
  waiting for transfers between devices: 21.9 us -> 15.6 us
  Pallas kernels: 10.6 us -> 6.15 us
  starting transfers between devices: 7.01 us -> 9.32 us
  other arithmetic: 1.01 us -> 1.89 us
  local copies, waits for them, and re-layouts: 0.03 us -> 0.86 us
    pallas_call x3, Pallas kernels: 10.6 us -> 6.15 us  [the longest x2 3.3 us: stop_call(): pl.pallas_call(functools.partial(stop_kernel, which, following), out_shap...]
    ppermute x5, waiting for transfers between devices: 7.34 us -> 3.83 us  [swap(): lax.ppermute(block, 'rep', [(r, r ^ bit) for r in range(lax.axis_size('re...]
    ppermute x2 -> x3, waiting for transfers between devices: 14.6 us -> 11.7 us  [joint(): return lax.ppermute(block, ('blk', 'rep'), route)]
    ppermute x5, starting transfers between devices: 1.85 us -> 3.19 us  [swap(): lax.ppermute(block, 'rep', [(r, r ^ bit) for r in range(lax.axis_size('re...]
    ppermute x2 -> x3, starting transfers between devices: 5.16 us -> 6.13 us  [joint(): return lax.ppermute(block, ('blk', 'rep'), route)]
    convert_element_type x2 -> x3, other arithmetic: 0.11 us -> 0.97 us  [the longest x1 0.81 us: on_device(): (users32 - rate_user * (total + shrinkage * users32)).astype(users.dtype)]
    dynamic_slice x1, local copies, waits for them, and re-layouts: 0.03 us -> 0.73 us  [half_of(): return lax.dynamic_slice_in_dim(array, c * half, half)]
  transfers between devices with their start and end apart: 7 -> 8, of which waited for: 5 -> 4; matrix products, arithmetic and copies ran while one was open for 0% -> 5% of each run, Pallas kernels for 26% -> 18%
where the time goes in v2:
time: 34.9 us; the launch traced here: 34.5 us
  waiting for transfers between devices  15.6 us (45%)
  starting transfers between devices  9.32 us (27%)
  Pallas kernels  6.15 us (18%)
  other arithmetic  1.89 us (5%)
  local copies, waits for them, and re-layouts  0.86 us (2%)
  between operations  0.74 us (2%)
    ppermute x3, waiting for transfers between devices, joint(): return lax.ppermute(block, ('blk', 'rep'), route)  11.7 us
    ppermute x3, starting transfers between devices, joint(): return lax.ppermute(block, ('blk', 'rep'), route)  6.13 us
    ppermute x5, waiting for transfers between devices, swap(): lax.ppermute(block, 'rep', [(r, r ^ bit) for r in range(lax.axis_size('re...  3.83 us
    pallas_call x2, Pallas kernels, stop_call(): pl.pallas_call(functools.partial(stop_kernel, which, following), out_shap...  3.3 us
    ppermute x5, starting transfers between devices, swap(): lax.ppermute(block, 'rep', [(r, r ^ bit) for r in range(lax.axis_size('re...  3.19 us
    pallas_call x1, Pallas kernels, own_call(): pl.pallas_call(own_kernel, out_shape=(shape(users.shape, f32), shape((n_i...  2.84 us
    convert_element_type x1, other arithmetic, on_device(): (users32 - rate_user * (total + shrinkage * users32)).astype(users.dtype)  0.81 us
    dynamic_slice x1, local copies, waits for them, and re-layouts, half_of(): return lax.dynamic_slice_in_dim(array, c * half, half)  0.73 us
  transfers between devices with their start and end apart: 8, of which 4 were waited for; matrix products, arithmetic and copies ran while one was open for 5% of the time, Pallas kernels for 18%

profile of v2, /device:TPU:0, one launch (start us, length us, event | category | flops | bytes accessed | tf_op | source)
XLA Modules:
  0.0 34.5 jit_solution(17430504238076847692)
XLA Ops:
  0.6 5.1 %collective-permute-start = (bf16[1024,128]{1,0:T(8,128)(2,1)}, bf16[1024,128]{1,0:T(8,128)(2,1)S(1)}, u32[]{:S(2)}, u32[]{:S(2)}) collective-permute-start(bf16[1024,128]{1,0:T(8,128)(2,1)} %items.1), channel_id=1, source_target_pairs={{0,24},{1,29},{2,26},{3,31},{4,28},{5,1},{6,30},{7,3},{8,0},{9,5},... | collective-permute-start | bytes 786440 | tf_op jit(solution)/shard_map/ppermute | solution.py:233
  5.7 2.8 %shard_map.77 = (f32[1024,128]{1,0:T(8,128)S(1)}, f32[8,128,128]{2,1,0:T(8,128)S(1)}, bf16[40,128,128]{2,1,0:T(8,128)(2,1)S(1)}, bf16[1024,128]{1,0:T(8,128)(2,1...) custom-call(s32[1,1,3]{2,1,0:T(1,128)} %counts.1, ...), custom_call_target="tpu_custom_call" | custom-call | flops 10000000000 | bytes 8000000 | tf_op jit(solution)/shard_map/pallas_call | solution.py:138
  8.6 0.7 %constant_dynamic-slice_fusion = f32[4,128,128]{2,1,0:T(8,128)} fusion(f32[8,128,128]{2,1,0:T(8,128)S(1)} %get-tuple-element.25, s32[]{:T(128)S(6)} %select_n.26), kind=kLoop, calls=%fused_computation.17 | loop fusion | bytes 524292 | tf_op jit(solution)/shard_map/dynamic_slice | solution.py:265
  9.3 0.0 collective-permute-start.2
  9.3 3.2 %collective-permute-done.refs_5_ = bf16[1024,128]{1,0:T(8,128)(2,1)S(1)} collective-permute-done((bf16[1024,128]{1,0:T(8,128)(2,1)}, bf16[1024,128]{1,0:T(8,128)(2,1)S(1)}, u32[]{:S(2)}, u32[]{:S(2)}) %collective-permute-start) | collective-permute-done | bytes 262176 | tf_op jit(solution)/shard_map/ppermute | solution.py:233
  12.6 0.0 collective-permute-start.1
  12.6 1.7 %shard_map.78 = (f32[1024,128]{1,0:T(8,128)S(1)}, f32[8,128,128]{2,1,0:T(8,128)S(1)}, bf16[40,128,128]{2,1,0:T(8,128)(2,1)S(1)}) custom-call(s32[1,1,3]{2,1,0:T(1,128)S(1)} %get-tuple-element.16.refs_0_, s32[1,3,1,40]{3,2,1,0:T(1,128)S(1)} %get-tuple-element.17.refs_1_, ...), custom_call_target="tpu_custom_call", output_to_operand_aliasing={{0}: (7, {})} | custom-call | flops 10000000000 | bytes 8000000 | tf_op jit(solution)/shard_map/pallas_call | solution.py:214
  14.3 0.5 %collective-permute-start.3 = (f32[8,128,128]{2,1,0:T(8,128)S(1)}, f32[8,128,128]{2,1,0:T(8,128)S(1)}, u32[]{:S(2)}, u32[]{:S(2)}) collective-permute-start(f32[8,128,128]{2,1,0:T(8,128)S(1)} %get-tuple-element.27), channel_id=1, source_target_pairs={{0,1},{1,0},{2,3},{3,2},{4,5},{5,4},{6,7},{7,6},{8,9},{9,8},{10,11... | collective-permute-start | bytes 1572872 | tf_op jit(solution)/shard_map/ppermute | solution.py:237
  14.8 0.0 collective-permute-done.1.refs_5_
  14.8 1.6 %shard_map.79 = (f32[1024,128]{1,0:T(8,128)S(1)}, f32[8,128,128]{2,1,0:T(8,128)S(1)}) custom-call(s32[1,1,3]{2,1,0:T(1,128)S(1)} %get-tuple-element.16.refs_0_, s32[1,3,1,40]{3,2,1,0:T(1,128)S(1)} %get-tuple-element.17.refs_1_, s32[1,3,1,40]{3,2,1,0:T(1,128)S(1)} %get-tuple-element.18.refs_2_, ...), custom_call_target="tpu_custom_call", output_to_operand_aliasing={{0}: (7, {})} | custom-call | flops 10000000000 | bytes 8000000 | tf_op jit(solution)/shard_map/pallas_call | solution.py:214
  16.4 0.0 collective-permute-done.3
  16.4 0.1 add.37
  16.5 0.0 copy-start
  16.5 0.1 multiply_convert_fusion.2
  16.6 0.1 collective-permute-start.4
  16.6 1.0 %collective-permute-start.5 = (f16[4,128,128]{2,1,0:T(8,128)(2,1)S(1)}, f16[4,128,128]{2,1,0:T(8,128)(2,1)S(1)}, u32[]{:S(2)}, u32[]{:S(2)}) collective-permute-start(f16[4,128,128]{2,1,0:T(8,128)(2,1)S(1)} %get-tuple-element.29), channel_id=1, source_target_pairs={{0,5},{1,8},{2,7},{3,10},{4,9},{5,12},{6,11},{7,14},{8,13},{9,16},... | collective-permute-start | bytes 393224 | tf_op jit(solution)/shard_map/ppermute | solution.py:233
  17.6 0.0 collective-permute-done.2
  17.6 8.5 %collective-permute-done.4 = f16[4,128,128]{2,1,0:T(8,128)(2,1)S(1)} collective-permute-done((f16[4,128,128]{2,1,0:T(8,128)(2,1)S(1)}, f16[4,128,128]{2,1,0:T(8,128)(2,1)S(1)}, u32[]{:S(2)}, u32[]{:S(2)}) %collective-permute-start.4) | collective-permute-done | bytes 131104 | tf_op jit(solution)/shard_map/ppermute | solution.py:233
  26.1 0.0 collective-permute-done.5
  26.1 0.1 multiply_convert_fusion
  26.2 1.9 %collective-permute-start.6 = (f16[4,128,128]{2,1,0:T(8,128)(2,1)S(1)}, f16[4,128,128]{2,1,0:T(8,128)(2,1)S(1)}, u32[]{:S(2)}, u32[]{:S(2)}) collective-permute-start(f16[4,128,128]{2,1,0:T(8,128)(2,1)S(1)} %multiply_convert_fusion), channel_id=1, source_target_pairs={{0,2},{1,3},{2,0},{3,1},{4,6},{5,7},{6,4},{7,5},{8,10},{9,11},{10,... | collective-permute-start | bytes 393224 | tf_op jit(solution)/shard_map/ppermute | solution.py:237
  28.1 3.6 %collective-permute-done.6 = f16[4,128,128]{2,1,0:T(8,128)(2,1)S(1)} collective-permute-done((f16[4,128,128]{2,1,0:T(8,128)(2,1)S(1)}, f16[4,128,128]{2,1,0:T(8,128)(2,1)S(1)}, u32[]{:S(2)}, u32[]{:S(2)}) %collective-permute-start.6) | collective-permute-done | bytes 131104 | tf_op jit(solution)/shard_map/ppermute | solution.py:237
  31.8 0.1 copy.10
  31.9 0.0 copy-done
  32.0 0.1 fusion.5
  32.0 0.7 %collective-permute-start.7 = (bf16[512,128]{1,0:T(8,128)(2,1)S(1)}, bf16[512,128]{1,0:T(8,128)(2,1)S(1)}, u32[]{:S(2)}, u32[]{:S(2)}) collective-permute-start(bf16[512,128]{1,0:T(8,128)(2,1)S(1)} %fusion.5), channel_id=1, source_target_pairs={{0,1},{1,0},{2,3},{3,2},{4,5},{5,4},{6,7},{7,6},{8,9},{9,8},{10,11... | collective-permute-start | bytes 393224 | tf_op jit(solution)/shard_map/ppermute | solution.py:237
  32.8 0.8 %fusion.2 = bf16[1024,128]{1,0:T(8,128)(2,1)} fusion(f32[1024,128]{1,0:T(8,128)S(1)} %get-tuple-element.24, bf16[1024,128]{1,0:T(8,128)(2,1)S(1)} %get-tuple-element.15.refs_3_), kind=kLoop, calls=%fused_computation.4 | loop fusion | flops 786432 | bytes 1048576 | tf_op jit(solution)/shard_map/convert_element_type | solution.py:260
  33.6 0.2 collective-permute-done.7
  33.8 0.7 %pad_maximum_fusion = bf16[1024,128]{1,0:T(8,128)(2,1)} fusion(bf16[512,128]{1,0:T(8,128)(2,1)S(1)} %get-tuple-element.31, bf16[512,128]{1,0:T(8,128)(2,1)S(1)} %get-tuple-element.30), kind=kLoop, calls=%fused_computation.10 | loop fusion | flops 524288 | bytes 524288 | tf_op jit(solution)/shard_map/concatenate | solution.py:283
  (2 shorter events, 0.1 us)
Async XLA Ops:
  0.6 11.9 %collective-permute-start = (bf16[1024,128]{1,0:T(8,128)(2,1)}, bf16[1024,128]{1,0:T(8,128)(2,1)S(1)}, u32[]{:S(2)}, u32[]{:S(2)}) collective-permute-start(bf16[1024,128]{1,0:T(8,128)(2,1)} %items.1), channel_id=1, source_target_pairs={{0,24},{1,29},{2,26},{3,31},{4,28},{5,1},{6,30},{7,3},{8,0},{9,5},... | collective-permute-start | bytes 786440 | tf_op jit(solution)/shard_map/ppermute | solution.py:233
  9.3 8.3 %collective-permute-start.2 = (f32[4,128,128]{2,1,0:T(8,128)}, f32[4,128,128]{2,1,0:T(8,128)S(1)}, u32[]{:S(2)}, u32[]{:S(2)}) collective-permute-start(f32[4,128,128]{2,1,0:T(8,128)} %constant_dynamic-slice_fusion), channel_id=1, source_target_pairs={{0,1},{1,0},{2,3},{3,2},{4,5},{5,4},{6,7},{7,6},{8,9},{9,8},{10,11... | collective-permute-start | bytes 786440 | tf_op jit(solution)/shard_map/ppermute | solution.py:237
  12.6 2.2 %collective-permute-start.1 = (bf16[1024,128]{1,0:T(8,128)(2,1)S(1)}, bf16[1024,128]{1,0:T(8,128)(2,1)S(1)}, u32[]{:S(2)}, u32[]{:S(2)}) collective-permute-start(bf16[1024,128]{1,0:T(8,128)(2,1)S(1)} %collective-permute-done.refs_5_), channel_id=1, source_target_pairs={{0,1},{1,0},{2,3},{3,2},{4,5},{5,4},{6,7},{7,6},{8,9},{9,8},{10,11... | collective-permute-start | bytes 786440 | tf_op jit(solution)/shard_map/ppermute | solution.py:237
  14.3 2.1 %collective-permute-start.3 = (f32[8,128,128]{2,1,0:T(8,128)S(1)}, f32[8,128,128]{2,1,0:T(8,128)S(1)}, u32[]{:S(2)}, u32[]{:S(2)}) collective-permute-start(f32[8,128,128]{2,1,0:T(8,128)S(1)} %get-tuple-element.27), channel_id=1, source_target_pairs={{0,1},{1,0},{2,3},{3,2},{4,5},{5,4},{6,7},{7,6},{8,9},{9,8},{10,11... | collective-permute-start | bytes 1572872 | tf_op jit(solution)/shard_map/ppermute | solution.py:237
  16.5 15.5 %copy-start = (bf16[1024,128]{1,0:T(8,128)(2,1)S(1)}, bf16[1024,128]{1,0:T(8,128)(2,1)}, u32[]{:S(2)}) copy-start(bf16[1024,128]{1,0:T(8,128)(2,1)} %items.1) | copy-start | bytes 786436
  16.6 9.5 %collective-permute-start.4 = (f16[4,128,128]{2,1,0:T(8,128)(2,1)S(1)}, f16[4,128,128]{2,1,0:T(8,128)(2,1)S(1)}, u32[]{:S(2)}, u32[]{:S(2)}) collective-permute-start(f16[4,128,128]{2,1,0:T(8,128)(2,1)S(1)} %get-tuple-element.28), channel_id=1, source_target_pairs={{0,4},{1,9},{2,6},{3,11},{4,8},{5,13},{6,10},{7,15},{8,12},{9,17},... | collective-permute-start | bytes 393224 | tf_op jit(solution)/shard_map/ppermute | solution.py:233
  16.6 9.5 %collective-permute-start.5 = (f16[4,128,128]{2,1,0:T(8,128)(2,1)S(1)}, f16[4,128,128]{2,1,0:T(8,128)(2,1)S(1)}, u32[]{:S(2)}, u32[]{:S(2)}) collective-permute-start(f16[4,128,128]{2,1,0:T(8,128)(2,1)S(1)} %get-tuple-element.29), channel_id=1, source_target_pairs={{0,5},{1,8},{2,7},{3,10},{4,9},{5,12},{6,11},{7,14},{8,13},{9,16},... | collective-permute-start | bytes 393224 | tf_op jit(solution)/shard_map/ppermute | solution.py:233
  26.2 5.6 %collective-permute-start.6 = (f16[4,128,128]{2,1,0:T(8,128)(2,1)S(1)}, f16[4,128,128]{2,1,0:T(8,128)(2,1)S(1)}, u32[]{:S(2)}, u32[]{:S(2)}) collective-permute-start(f16[4,128,128]{2,1,0:T(8,128)(2,1)S(1)} %multiply_convert_fusion), channel_id=1, source_target_pairs={{0,2},{1,3},{2,0},{3,1},{4,6},{5,7},{6,4},{7,5},{8,10},{9,11},{10,... | collective-permute-start | bytes 393224 | tf_op jit(solution)/shard_map/ppermute | solution.py:237
  32.0 1.7 %collective-permute-start.7 = (bf16[512,128]{1,0:T(8,128)(2,1)S(1)}, bf16[512,128]{1,0:T(8,128)(2,1)S(1)}, u32[]{:S(2)}, u32[]{:S(2)}) collective-permute-start(bf16[512,128]{1,0:T(8,128)(2,1)S(1)} %fusion.5), channel_id=1, source_target_pairs={{0,1},{1,0},{2,3},{3,2},{4,5},{5,4},{6,7},{7,6},{8,9},{9,8},{10,11... | collective-permute-start | bytes 393224 | tf_op jit(solution)/shard_map/ppermute | solution.py:237

commit v3 on v2

--- a/solution.py
+++ b/solution.py
@@ -12,7 +12,7 @@
 shrinkage = 0.05
 step_gain = 0.3
 chunk = 8
-group = 8
+group = 20
 cores = 2
 f32, bf16, f16 = jnp.float32, jnp.bfloat16, jnp.float16
 

time: 34.9 us -> 35.7 us (1.023)
  Pallas kernels: 6.15 us -> 7.4 us
  waiting for transfers between devices: 15.6 us -> 15.2 us
    pallas_call x1, Pallas kernels: 2.84 us -> 4.03 us  [own_call(): pl.pallas_call(own_kernel, out_shape=(shape(users.shape, f32), shape((n_i...]
    ppermute x3, waiting for transfers between devices: 11.7 us -> 11.1 us  [joint(): return lax.ppermute(block, ('blk', 'rep'), route)]
  transfers between devices with their start and end apart: 8 -> 8, of which waited for: 4 -> 4; matrix products, arithmetic and copies ran while one was open for 5% -> 5% of each run, Pallas kernels for 18% -> 21%
where the time goes in v3:
time: 35.7 us; the launch traced here: 35.1 us
  waiting for transfers between devices  15.2 us (43%)
  starting transfers between devices  9.02 us (25%)
  Pallas kernels  7.4 us (21%)
  other arithmetic  1.89 us (5%)
  local copies, waits for them, and re-layouts  0.86 us (2%)
  between operations  0.73 us (2%)
    ppermute x3, waiting for transfers between devices, joint(): return lax.ppermute(block, ('blk', 'rep'), route)  11.1 us
    ppermute x3, starting transfers between devices, joint(): return lax.ppermute(block, ('blk', 'rep'), route)  6.01 us
    ppermute x5, waiting for transfers between devices, swap(): lax.ppermute(block, 'rep', [(r, r ^ bit) for r in range(lax.axis_size('re...  4.14 us
    pallas_call x1, Pallas kernels, own_call(): pl.pallas_call(own_kernel, out_shape=(shape(users.shape, f32), shape((n_i...  4.03 us
    pallas_call x2, Pallas kernels, stop_call(): pl.pallas_call(functools.partial(stop_kernel, which, following), out_shap...  3.37 us
    ppermute x5, starting transfers between devices, swap(): lax.ppermute(block, 'rep', [(r, r ^ bit) for r in range(lax.axis_size('re...  3.01 us
    convert_element_type x1, other arithmetic, on_device(): (users32 - rate_user * (total + shrinkage * users32)).astype(users.dtype)  0.81 us
    dynamic_slice x1, local copies, waits for them, and re-layouts, half_of(): return lax.dynamic_slice_in_dim(array, c * half, half)  0.73 us
  transfers between devices with their start and end apart: 8, of which 4 were waited for; matrix products, arithmetic and copies ran while one was open for 5% of the time, Pallas kernels for 21%

profile of v3, /device:TPU:0, one launch (start us, length us, event | category | flops | bytes accessed | tf_op | source)
XLA Modules:
  0.0 35.1 jit_solution(14048831900661344155)
XLA Ops:
  0.6 5.1 %collective-permute-start = (bf16[1024,128]{1,0:T(8,128)(2,1)}, bf16[1024,128]{1,0:T(8,128)(2,1)S(1)}, u32[]{:S(2)}, u32[]{:S(2)}) collective-permute-start(bf16[1024,128]{1,0:T(8,128)(2,1)} %items.1), channel_id=1, source_target_pairs={{0,24},{1,29},{2,26},{3,31},{4,28},{5,1},{6,30},{7,3},{8,0},{9,5},... | collective-permute-start | bytes 786440 | tf_op jit(solution)/shard_map/ppermute | solution.py:233
  5.7 4.0 %shard_map.77 = (f32[1024,128]{1,0:T(8,128)S(1)}, f32[8,128,128]{2,1,0:T(8,128)S(1)}, bf16[40,128,128]{2,1,0:T(8,128)(2,1)S(1)}, bf16[1024,128]{1,0:T(8,128)(2,1...) custom-call(s32[1,1,3]{2,1,0:T(1,128)} %counts.1, ...), custom_call_target="tpu_custom_call" | custom-call | flops 10000000000 | bytes 8000000 | tf_op jit(solution)/shard_map/pallas_call | solution.py:138
  9.8 0.7 %constant_dynamic-slice_fusion = f32[4,128,128]{2,1,0:T(8,128)} fusion(f32[8,128,128]{2,1,0:T(8,128)S(1)} %get-tuple-element.25, s32[]{:T(128)S(6)} %select_n.26), kind=kLoop, calls=%fused_computation.17 | loop fusion | bytes 524292 | tf_op jit(solution)/shard_map/dynamic_slice | solution.py:265
  10.5 0.0 collective-permute-start.2
  10.5 2.1 %collective-permute-done.refs_5_ = bf16[1024,128]{1,0:T(8,128)(2,1)S(1)} collective-permute-done((bf16[1024,128]{1,0:T(8,128)(2,1)}, bf16[1024,128]{1,0:T(8,128)(2,1)S(1)}, u32[]{:S(2)}, u32[]{:S(2)}) %collective-permute-start) | collective-permute-done | bytes 262176 | tf_op jit(solution)/shard_map/ppermute | solution.py:233
  12.6 0.0 collective-permute-start.1
  12.6 1.7 %shard_map.78 = (f32[1024,128]{1,0:T(8,128)S(1)}, f32[8,128,128]{2,1,0:T(8,128)S(1)}, bf16[40,128,128]{2,1,0:T(8,128)(2,1)S(1)}) custom-call(s32[1,1,3]{2,1,0:T(1,128)S(1)} %get-tuple-element.16.refs_0_, s32[1,3,1,40]{3,2,1,0:T(1,128)S(1)} %get-tuple-element.17.refs_1_, ...), custom_call_target="tpu_custom_call", output_to_operand_aliasing={{0}: (7, {})} | custom-call | flops 10000000000 | bytes 8000000 | tf_op jit(solution)/shard_map/pallas_call | solution.py:214
  14.3 0.6 %collective-permute-start.3 = (f32[8,128,128]{2,1,0:T(8,128)S(1)}, f32[8,128,128]{2,1,0:T(8,128)S(1)}, u32[]{:S(2)}, u32[]{:S(2)}) collective-permute-start(f32[8,128,128]{2,1,0:T(8,128)S(1)} %get-tuple-element.27), channel_id=1, source_target_pairs={{0,1},{1,0},{2,3},{3,2},{4,5},{5,4},{6,7},{7,6},{8,9},{9,8},{10,11... | collective-permute-start | bytes 1572872 | tf_op jit(solution)/shard_map/ppermute | solution.py:237
  14.9 0.0 collective-permute-done.1.refs_5_
  14.9 1.7 %shard_map.79 = (f32[1024,128]{1,0:T(8,128)S(1)}, f32[8,128,128]{2,1,0:T(8,128)S(1)}) custom-call(s32[1,1,3]{2,1,0:T(1,128)S(1)} %get-tuple-element.16.refs_0_, s32[1,3,1,40]{3,2,1,0:T(1,128)S(1)} %get-tuple-element.17.refs_1_, s32[1,3,1,40]{3,2,1,0:T(1,128)S(1)} %get-tuple-element.18.refs_2_, ...), custom_call_target="tpu_custom_call", output_to_operand_aliasing={{0}: (7, {})} | custom-call | flops 10000000000 | bytes 8000000 | tf_op jit(solution)/shard_map/pallas_call | solution.py:214
  16.5 0.0 collective-permute-done.3
  16.5 0.1 add.37
  16.6 0.0 copy-start
  16.6 0.1 multiply_convert_fusion.2
  16.7 0.5 %collective-permute-start.4 = (f16[4,128,128]{2,1,0:T(8,128)(2,1)S(1)}, f16[4,128,128]{2,1,0:T(8,128)(2,1)S(1)}, u32[]{:S(2)}, u32[]{:S(2)}) collective-permute-start(f16[4,128,128]{2,1,0:T(8,128)(2,1)S(1)} %get-tuple-element.28), channel_id=1, source_target_pairs={{0,4},{1,9},{2,6},{3,11},{4,8},{5,13},{6,10},{7,15},{8,12},{9,17},... | collective-permute-start | bytes 393224 | tf_op jit(solution)/shard_map/ppermute | solution.py:233
  17.2 0.4 %collective-permute-start.5 = (f16[4,128,128]{2,1,0:T(8,128)(2,1)S(1)}, f16[4,128,128]{2,1,0:T(8,128)(2,1)S(1)}, u32[]{:S(2)}, u32[]{:S(2)}) collective-permute-start(f16[4,128,128]{2,1,0:T(8,128)(2,1)S(1)} %get-tuple-element.29), channel_id=1, source_target_pairs={{0,5},{1,8},{2,7},{3,10},{4,9},{5,12},{6,11},{7,14},{8,13},{9,16},... | collective-permute-start | bytes 393224 | tf_op jit(solution)/shard_map/ppermute | solution.py:233
  17.6 0.0 collective-permute-done.2
  17.6 9.0 %collective-permute-done.4 = f16[4,128,128]{2,1,0:T(8,128)(2,1)S(1)} collective-permute-done((f16[4,128,128]{2,1,0:T(8,128)(2,1)S(1)}, f16[4,128,128]{2,1,0:T(8,128)(2,1)S(1)}, u32[]{:S(2)}, u32[]{:S(2)}) %collective-permute-start.4) | collective-permute-done | bytes 131104 | tf_op jit(solution)/shard_map/ppermute | solution.py:233
  26.6 0.0 collective-permute-done.5
  26.6 0.1 multiply_convert_fusion
  26.7 2.1 %collective-permute-start.6 = (f16[4,128,128]{2,1,0:T(8,128)(2,1)S(1)}, f16[4,128,128]{2,1,0:T(8,128)(2,1)S(1)}, u32[]{:S(2)}, u32[]{:S(2)}) collective-permute-start(f16[4,128,128]{2,1,0:T(8,128)(2,1)S(1)} %multiply_convert_fusion), channel_id=1, source_target_pairs={{0,2},{1,3},{2,0},{3,1},{4,6},{5,7},{6,4},{7,5},{8,10},{9,11},{10,... | collective-permute-start | bytes 393224 | tf_op jit(solution)/shard_map/ppermute | solution.py:237
  28.8 3.9 %collective-permute-done.6 = f16[4,128,128]{2,1,0:T(8,128)(2,1)S(1)} collective-permute-done((f16[4,128,128]{2,1,0:T(8,128)(2,1)S(1)}, f16[4,128,128]{2,1,0:T(8,128)(2,1)S(1)}, u32[]{:S(2)}, u32[]{:S(2)}) %collective-permute-start.6) | collective-permute-done | bytes 131104 | tf_op jit(solution)/shard_map/ppermute | solution.py:237
  32.7 0.1 copy.10
  32.9 0.0 copy-done
  32.9 0.1 fusion.5
  33.0 0.4 %collective-permute-start.7 = (bf16[512,128]{1,0:T(8,128)(2,1)S(1)}, bf16[512,128]{1,0:T(8,128)(2,1)S(1)}, u32[]{:S(2)}, u32[]{:S(2)}) collective-permute-start(bf16[512,128]{1,0:T(8,128)(2,1)S(1)} %fusion.5), channel_id=1, source_target_pairs={{0,1},{1,0},{2,3},{3,2},{4,5},{5,4},{6,7},{7,6},{8,9},{9,8},{10,11... | collective-permute-start | bytes 393224 | tf_op jit(solution)/shard_map/ppermute | solution.py:237
  33.3 0.8 %fusion.2 = bf16[1024,128]{1,0:T(8,128)(2,1)} fusion(f32[1024,128]{1,0:T(8,128)S(1)} %get-tuple-element.24, bf16[1024,128]{1,0:T(8,128)(2,1)S(1)} %get-tuple-element.15.refs_3_), kind=kLoop, calls=%fused_computation.4 | loop fusion | flops 786432 | bytes 1048576 | tf_op jit(solution)/shard_map/convert_element_type | solution.py:260
  34.1 0.2 collective-permute-done.7
  34.4 0.7 %pad_maximum_fusion = bf16[1024,128]{1,0:T(8,128)(2,1)} fusion(bf16[512,128]{1,0:T(8,128)(2,1)S(1)} %get-tuple-element.31, bf16[512,128]{1,0:T(8,128)(2,1)S(1)} %get-tuple-element.30), kind=kLoop, calls=%fused_computation.10 | loop fusion | flops 524288 | bytes 524288 | tf_op jit(solution)/shard_map/concatenate | solution.py:283
  (2 shorter events, 0.1 us)
Async XLA Ops:
  0.6 11.9 %collective-permute-start = (bf16[1024,128]{1,0:T(8,128)(2,1)}, bf16[1024,128]{1,0:T(8,128)(2,1)S(1)}, u32[]{:S(2)}, u32[]{:S(2)}) collective-permute-start(bf16[1024,128]{1,0:T(8,128)(2,1)} %items.1), channel_id=1, source_target_pairs={{0,24},{1,29},{2,26},{3,31},{4,28},{5,1},{6,30},{7,3},{8,0},{9,5},... | collective-permute-start | bytes 786440 | tf_op jit(solution)/shard_map/ppermute | solution.py:233
  10.5 7.1 %collective-permute-start.2 = (f32[4,128,128]{2,1,0:T(8,128)}, f32[4,128,128]{2,1,0:T(8,128)S(1)}, u32[]{:S(2)}, u32[]{:S(2)}) collective-permute-start(f32[4,128,128]{2,1,0:T(8,128)} %constant_dynamic-slice_fusion), channel_id=1, source_target_pairs={{0,1},{1,0},{2,3},{3,2},{4,5},{5,4},{6,7},{7,6},{8,9},{9,8},{10,11... | collective-permute-start | bytes 786440 | tf_op jit(solution)/shard_map/ppermute | solution.py:237
  12.6 2.3 %collective-permute-start.1 = (bf16[1024,128]{1,0:T(8,128)(2,1)S(1)}, bf16[1024,128]{1,0:T(8,128)(2,1)S(1)}, u32[]{:S(2)}, u32[]{:S(2)}) collective-permute-start(bf16[1024,128]{1,0:T(8,128)(2,1)S(1)} %collective-permute-done.refs_5_), channel_id=1, source_target_pairs={{0,1},{1,0},{2,3},{3,2},{4,5},{5,4},{6,7},{7,6},{8,9},{9,8},{10,11... | collective-permute-start | bytes 786440 | tf_op jit(solution)/shard_map/ppermute | solution.py:237
  14.3 2.3 %collective-permute-start.3 = (f32[8,128,128]{2,1,0:T(8,128)S(1)}, f32[8,128,128]{2,1,0:T(8,128)S(1)}, u32[]{:S(2)}, u32[]{:S(2)}) collective-permute-start(f32[8,128,128]{2,1,0:T(8,128)S(1)} %get-tuple-element.27), channel_id=1, source_target_pairs={{0,1},{1,0},{2,3},{3,2},{4,5},{5,4},{6,7},{7,6},{8,9},{9,8},{10,11... | collective-permute-start | bytes 1572872 | tf_op jit(solution)/shard_map/ppermute | solution.py:237
  16.6 16.2 %copy-start = (bf16[1024,128]{1,0:T(8,128)(2,1)S(1)}, bf16[1024,128]{1,0:T(8,128)(2,1)}, u32[]{:S(2)}) copy-start(bf16[1024,128]{1,0:T(8,128)(2,1)} %items.1) | copy-start | bytes 786436
  16.7 9.9 %collective-permute-start.4 = (f16[4,128,128]{2,1,0:T(8,128)(2,1)S(1)}, f16[4,128,128]{2,1,0:T(8,128)(2,1)S(1)}, u32[]{:S(2)}, u32[]{:S(2)}) collective-permute-start(f16[4,128,128]{2,1,0:T(8,128)(2,1)S(1)} %get-tuple-element.28), channel_id=1, source_target_pairs={{0,4},{1,9},{2,6},{3,11},{4,8},{5,13},{6,10},{7,15},{8,12},{9,17},... | collective-permute-start | bytes 393224 | tf_op jit(solution)/shard_map/ppermute | solution.py:233
  17.2 9.4 %collective-permute-start.5 = (f16[4,128,128]{2,1,0:T(8,128)(2,1)S(1)}, f16[4,128,128]{2,1,0:T(8,128)(2,1)S(1)}, u32[]{:S(2)}, u32[]{:S(2)}) collective-permute-start(f16[4,128,128]{2,1,0:T(8,128)(2,1)S(1)} %get-tuple-element.29), channel_id=1, source_target_pairs={{0,5},{1,8},{2,7},{3,10},{4,9},{5,12},{6,11},{7,14},{8,13},{9,16},... | collective-permute-start | bytes 393224 | tf_op jit(solution)/shard_map/ppermute | solution.py:233
  26.7 6.0 %collective-permute-start.6 = (f16[4,128,128]{2,1,0:T(8,128)(2,1)S(1)}, f16[4,128,128]{2,1,0:T(8,128)(2,1)S(1)}, u32[]{:S(2)}, u32[]{:S(2)}) collective-permute-start(f16[4,128,128]{2,1,0:T(8,128)(2,1)S(1)} %multiply_convert_fusion), channel_id=1, source_target_pairs={{0,2},{1,3},{2,0},{3,1},{4,6},{5,7},{6,4},{7,5},{8,10},{9,11},{10,... | collective-permute-start | bytes 393224 | tf_op jit(solution)/shard_map/ppermute | solution.py:237
  33.0 1.4 %collective-permute-start.7 = (bf16[512,128]{1,0:T(8,128)(2,1)S(1)}, bf16[512,128]{1,0:T(8,128)(2,1)S(1)}, u32[]{:S(2)}, u32[]{:S(2)}) collective-permute-start(bf16[512,128]{1,0:T(8,128)(2,1)S(1)} %fusion.5), channel_id=1, source_target_pairs={{0,1},{1,0},{2,3},{3,2},{4,5},{5,4},{6,7},{7,6},{8,9},{9,8},{10,11... | collective-permute-start | bytes 393224 | tf_op jit(solution)/shard_map/ppermute | solution.py:237

commit v4 on v3

--- a/solution.py
+++ b/solution.py
@@ -13,6 +13,7 @@
 step_gain = 0.3
 chunk = 8
 group = 20
+rests = (8, 12, 16)
 cores = 2
 f32, bf16, f16 = jnp.float32, jnp.bfloat16, jnp.float16
 
@@ -39,22 +40,22 @@
 
 
 def steps(live, size):
-    return lax.div(live + size - 1, size)
+    return (live + size - 1) // size if isinstance(live, int) else lax.div(live + size - 1, size)
 
 
 def run_slots(live, stop, ut_s, it_s, users, users_t, block, tiles, total, item_t):
     tile = tiles.shape[-1]
 
-    def step(g, carry):
+    def work(first, size):
         slots_now = []
-        for k in range(group):
-            s = g * group + k
+        for k in range(size):
+            s = first + k
             listed = jnp.minimum(s, ut_s.shape[-1] - 1)
             u_index = ut_s[stop, 0, listed]
             i_index = it_s[stop, 0, listed]
             u = users[tile_rows(u_index, tile)]
             v = block[tile_rows(i_index, tile)]
-            r = tiles[s].astype(f32)
+            r = tiles[listed].astype(f32)
             e = (1.0 + confidence * r) * (r - mul(u, v, NT))
             e = jnp.where(s < live, e, 0.0).astype(bf16)
             slots_now.append((u_index, i_index, v, e))
@@ -62,15 +63,30 @@
         for a, b, to_user, to_item in terms:
             total[tile_rows(a, tile)] += to_user
             item_t[b] += to_item
+
+    def step(g, carry):
+        work(g * group, group)
         return carry
 
-    lax.fori_loop(0, steps(live, group), step, 0)
+    whole = lax.div(live, group)
+    left = live - whole * group
+    whole = whole + (left > rests[-1]).astype(jnp.int32)
+    lax.fori_loop(0, whole, step, 0)
+    below = 0
+    for size in rests:
+
+        @pl.when((left > below) & (left <= size))
+        def _(size=size):
+            work(whole * group, size)
+
+        below = size
 
 
 class Tiles:
     def __init__(self, ratings, stop, counts, place, sems):
         self.ratings, self.stop, self.place, self.sems = ratings, stop, place, sems
-        self.count = steps(counts[stop], chunk)
+        slots = ratings.shape[3] if counts is None else counts[stop]
+        self.count = steps(slots, chunk)
 
     def copy(self, g):
         rows = pl.ds(g * chunk, chunk)
@@ -177,13 +193,13 @@
     ]
     for copy in lists:
         copy.start()
+    core = lax.rem(lax.axis_index("rep"), cores)
+    if following is not None:
+        plan = Tiles(ratings, following(core), None, tiles_next, arrive)
+        plan.start()
     item_t[...] = jnp.zeros_like(item_t)
     for copy in lists:
         copy.wait()
-    core = lax.rem(lax.axis_index("rep"), cores)
-    if following is not None:
-        plan = Tiles(ratings, following(core), counts_s, tiles_next, arrive)
-        plan.start()
     stop = which(core)
     run_slots(counts_s[stop], stop, ut_s, it_s, users, users_t, block, tiles, total, item_t)
     if following is not None:
@@ -254,7 +270,7 @@
     )
     far = swap(near, 1)
     total, given, far_r = stop_call(near_stop, lists, users_v, users_t, near, near_r, total, far_stop, ratings)
-    taken = swap(given, 1)
+    taken = swap((given * scale).astype(f16), 1).astype(f32) * (1.0 / scale)
     total, kept = stop_call(far_stop, lists, users_v, users_t, far, far_r, total)
     users32 = users_v.astype(f32)
     user_new = (users32 - rate_user * (total + shrinkage * users32)).astype(users.dtype)

time: 35.7 us -> 34.5 us (0.966)
  starting transfers between devices: 9.02 us -> 11 us
  Pallas kernels: 7.4 us -> 5.79 us
  waiting for transfers between devices: 15.2 us -> 13.6 us
    pallas_call x1, Pallas kernels: 4.03 us -> 2.54 us  [own_call(): pl.pallas_call(own_kernel, out_shape=(shape(users.shape, f32), shape((n_i...]
    ppermute x3, waiting for transfers between devices: 11.1 us -> 9.61 us  [joint(): return lax.ppermute(block, ('blk', 'rep'), route)]
    ppermute x3, starting transfers between devices: 6.01 us -> 7.19 us  [joint(): return lax.ppermute(block, ('blk', 'rep'), route)]
    ppermute x5, starting transfers between devices: 3.01 us -> 3.83 us  [swap(): lax.ppermute(block, 'rep', [(r, r ^ bit) for r in range(lax.axis_size('re...]
  transfers between devices with their start and end apart: 8 -> 8, of which waited for: 4 -> 4; matrix products, arithmetic and copies ran while one was open for 5% -> 5% of each run, Pallas kernels for 21% -> 17%
where the time goes in v4:
time: 34.5 us; the launch traced here: 33.9 us
  waiting for transfers between devices  13.6 us (39%)
  starting transfers between devices  11 us (32%)
  Pallas kernels  5.79 us (17%)
  other arithmetic  1.95 us (6%)
  local copies, waits for them, and re-layouts  0.86 us (2%)
  between operations  0.74 us (2%)
    ppermute x3, waiting for transfers between devices, joint(): return lax.ppermute(block, ('blk', 'rep'), route)  9.61 us
    ppermute x3, starting transfers between devices, joint(): return lax.ppermute(block, ('blk', 'rep'), route)  7.19 us
    ppermute x5, waiting for transfers between devices, swap(): lax.ppermute(block, 'rep', [(r, r ^ bit) for r in range(lax.axis_size('re...  3.94 us
    ppermute x5, starting transfers between devices, swap(): lax.ppermute(block, 'rep', [(r, r ^ bit) for r in range(lax.axis_size('re...  3.83 us
    pallas_call x2, Pallas kernels, stop_call(): pl.pallas_call(functools.partial(stop_kernel, which, following), out_shap...  3.25 us
    pallas_call x1, Pallas kernels, own_call(): pl.pallas_call(own_kernel, out_shape=(shape(users.shape, f32), shape((n_i...  2.54 us
    convert_element_type x1, other arithmetic, on_device(): (users32 - rate_user * (total + shrinkage * users32)).astype(users.dtype)  0.81 us
    dynamic_slice x1, local copies, waits for them, and re-layouts, half_of(): return lax.dynamic_slice_in_dim(array, c * half, half)  0.73 us
  transfers between devices with their start and end apart: 8, of which 4 were waited for; matrix products, arithmetic and copies ran while one was open for 5% of the time, Pallas kernels for 17%

profile of v4, /device:TPU:0, one launch (start us, length us, event | category | flops | bytes accessed | tf_op | source)
XLA Modules:
  0.0 33.9 jit_solution(14344680377801873342)
XLA Ops:
  0.6 5.1 %collective-permute-start = (bf16[1024,128]{1,0:T(8,128)(2,1)}, bf16[1024,128]{1,0:T(8,128)(2,1)S(1)}, u32[]{:S(2)}, u32[]{:S(2)}) collective-permute-start(bf16[1024,128]{1,0:T(8,128)(2,1)} %items.1), channel_id=1, source_target_pairs={{0,24},{1,29},{2,26},{3,31},{4,28},{5,1},{6,30},{7,3},{8,0},{9,5},... | collective-permute-start | bytes 786440 | tf_op jit(solution)/shard_map/ppermute | solution.py:249
  5.7 2.5 %shard_map.77 = (f32[1024,128]{1,0:T(8,128)S(1)}, f32[8,128,128]{2,1,0:T(8,128)S(1)}, bf16[40,128,128]{2,1,0:T(8,128)(2,1)S(1)}, bf16[1024,128]{1,0:T(8,128)(2,1...) custom-call(s32[1,1,3]{2,1,0:T(1,128)} %counts.1, ...), custom_call_target="tpu_custom_call" | custom-call | flops 10000000000 | bytes 8000000 | tf_op jit(solution)/shard_map/pallas_call | solution.py:154
  8.3 0.7 %constant_dynamic-slice_fusion = f32[4,128,128]{2,1,0:T(8,128)} fusion(f32[8,128,128]{2,1,0:T(8,128)S(1)} %get-tuple-element.25, s32[]{:T(128)S(6)} %select_n.26), kind=kLoop, calls=%fused_computation.19 | loop fusion | bytes 524292 | tf_op jit(solution)/shard_map/dynamic_slice | solution.py:281
  9.0 0.9 %collective-permute-start.2 = (f32[4,128,128]{2,1,0:T(8,128)}, f32[4,128,128]{2,1,0:T(8,128)S(1)}, u32[]{:S(2)}, u32[]{:S(2)}) collective-permute-start(f32[4,128,128]{2,1,0:T(8,128)} %constant_dynamic-slice_fusion), channel_id=1, source_target_pairs={{0,1},{1,0},{2,3},{3,2},{4,5},{5,4},{6,7},{7,6},{8,9},{9,8},{10,11... | collective-permute-start | bytes 786440 | tf_op jit(solution)/shard_map/ppermute | solution.py:253
  9.9 2.6 %collective-permute-done.refs_5_ = bf16[1024,128]{1,0:T(8,128)(2,1)S(1)} collective-permute-done((bf16[1024,128]{1,0:T(8,128)(2,1)}, bf16[1024,128]{1,0:T(8,128)(2,1)S(1)}, u32[]{:S(2)}, u32[]{:S(2)}) %collective-permute-start) | collective-permute-done | bytes 262176 | tf_op jit(solution)/shard_map/ppermute | solution.py:249
  12.6 0.0 collective-permute-start.1
  12.6 1.6 %shard_map.78 = (f32[1024,128]{1,0:T(8,128)S(1)}, f32[8,128,128]{2,1,0:T(8,128)S(1)}, bf16[40,128,128]{2,1,0:T(8,128)(2,1)S(1)}) custom-call(s32[1,1,3]{2,1,0:T(1,128)S(1)} %get-tuple-element.16.refs_0_, s32[1,3,1,40]{3,2,1,0:T(1,128)S(1)} %get-tuple-element.17.refs_1_, ...), custom_call_target="tpu_custom_call", output_to_operand_aliasing={{0}: (7, {})} | custom-call | flops 10000000000 | bytes 8000000 | tf_op jit(solution)/shard_map/pallas_call | solution.py:230
  14.1 0.1 multiply_convert_fusion
  14.2 0.3 %collective-permute-start.3 = (f16[8,128,128]{2,1,0:T(8,128)(2,1)S(1)}, f16[8,128,128]{2,1,0:T(8,128)(2,1)S(1)}, u32[]{:S(2)}, u32[]{:S(2)}) collective-permute-start(f16[8,128,128]{2,1,0:T(8,128)(2,1)S(1)} %multiply_convert_fusion), channel_id=1, source_target_pairs={{0,1},{1,0},{2,3},{3,2},{4,5},{5,4},{6,7},{7,6},{8,9},{9,8},{10,11... | collective-permute-start | bytes 786440 | tf_op jit(solution)/shard_map/ppermute | solution.py:253
  14.6 0.0 collective-permute-done.1.refs_5_
  14.6 1.7 %shard_map.79 = (f32[1024,128]{1,0:T(8,128)S(1)}, f32[8,128,128]{2,1,0:T(8,128)S(1)}) custom-call(s32[1,1,3]{2,1,0:T(1,128)S(1)} %get-tuple-element.16.refs_0_, s32[1,3,1,40]{3,2,1,0:T(1,128)S(1)} %get-tuple-element.17.refs_1_, s32[1,3,1,40]{3,2,1,0:T(1,128)S(1)} %get-tuple-element.18.refs_2_, ...), custom_call_target="tpu_custom_call", output_to_operand_aliasing={{0}: (7, {})} | custom-call | flops 10000000000 | bytes 8000000 | tf_op jit(solution)/shard_map/pallas_call | solution.py:230
  16.3 0.0 collective-permute-done.3
  16.3 0.1 multiply_add_fusion
  16.4 0.0 copy-start
  16.4 0.1 multiply_convert_fusion.3
  16.4 0.1 collective-permute-start.4
  16.5 2.0 %collective-permute-start.5 = (f16[4,128,128]{2,1,0:T(8,128)(2,1)S(1)}, f16[4,128,128]{2,1,0:T(8,128)(2,1)S(1)}, u32[]{:S(2)}, u32[]{:S(2)}) collective-permute-start(f16[4,128,128]{2,1,0:T(8,128)(2,1)S(1)} %get-tuple-element.29), channel_id=1, source_target_pairs={{0,5},{1,8},{2,7},{3,10},{4,9},{5,12},{6,11},{7,14},{8,13},{9,16},... | collective-permute-start | bytes 393224 | tf_op jit(solution)/shard_map/ppermute | solution.py:249
  18.5 0.0 collective-permute-done.2
  18.5 7.0 %collective-permute-done.4 = f16[4,128,128]{2,1,0:T(8,128)(2,1)S(1)} collective-permute-done((f16[4,128,128]{2,1,0:T(8,128)(2,1)S(1)}, f16[4,128,128]{2,1,0:T(8,128)(2,1)S(1)}, u32[]{:S(2)}, u32[]{:S(2)}) %collective-permute-start.4) | collective-permute-done | bytes 131104 | tf_op jit(solution)/shard_map/ppermute | solution.py:249
  25.5 0.0 collective-permute-done.5
  25.5 0.1 multiply_convert_fusion.1
  25.6 1.6 %collective-permute-start.6 = (f16[4,128,128]{2,1,0:T(8,128)(2,1)S(1)}, f16[4,128,128]{2,1,0:T(8,128)(2,1)S(1)}, u32[]{:S(2)}, u32[]{:S(2)}) collective-permute-start(f16[4,128,128]{2,1,0:T(8,128)(2,1)S(1)} %multiply_convert_fusion.1), channel_id=1, source_target_pairs={{0,2},{1,3},{2,0},{3,1},{4,6},{5,7},{6,4},{7,5},{8,10},{9,11},{10,... | collective-permute-start | bytes 393224 | tf_op jit(solution)/shard_map/ppermute | solution.py:253
  27.2 3.8 %collective-permute-done.6 = f16[4,128,128]{2,1,0:T(8,128)(2,1)S(1)} collective-permute-done((f16[4,128,128]{2,1,0:T(8,128)(2,1)S(1)}, f16[4,128,128]{2,1,0:T(8,128)(2,1)S(1)}, u32[]{:S(2)}, u32[]{:S(2)}) %collective-permute-start.6) | collective-permute-done | bytes 131104 | tf_op jit(solution)/shard_map/ppermute | solution.py:253
  31.0 0.1 copy.10
  31.2 0.0 copy-done
  31.2 0.1 fusion.5
  31.2 1.0 %collective-permute-start.7 = (bf16[512,128]{1,0:T(8,128)(2,1)S(1)}, bf16[512,128]{1,0:T(8,128)(2,1)S(1)}, u32[]{:S(2)}, u32[]{:S(2)}) collective-permute-start(bf16[512,128]{1,0:T(8,128)(2,1)S(1)} %fusion.5), channel_id=1, source_target_pairs={{0,1},{1,0},{2,3},{3,2},{4,5},{5,4},{6,7},{7,6},{8,9},{9,8},{10,11... | collective-permute-start | bytes 393224 | tf_op jit(solution)/shard_map/ppermute | solution.py:253
  32.2 0.8 %fusion.2 = bf16[1024,128]{1,0:T(8,128)(2,1)} fusion(f32[1024,128]{1,0:T(8,128)S(1)} %get-tuple-element.24, bf16[1024,128]{1,0:T(8,128)(2,1)S(1)} %get-tuple-element.15.refs_3_), kind=kLoop, calls=%fused_computation.4 | loop fusion | flops 786432 | bytes 1048576 | tf_op jit(solution)/shard_map/convert_element_type | solution.py:276
  33.0 0.2 collective-permute-done.7
  33.2 0.7 %pad_maximum_fusion = bf16[1024,128]{1,0:T(8,128)(2,1)} fusion(bf16[512,128]{1,0:T(8,128)(2,1)S(1)} %get-tuple-element.31, bf16[512,128]{1,0:T(8,128)(2,1)S(1)} %get-tuple-element.30), kind=kLoop, calls=%fused_computation.12 | loop fusion | flops 524288 | bytes 524288 | tf_op jit(solution)/shard_map/concatenate | solution.py:299
  (2 shorter events, 0.1 us)
Async XLA Ops:
  0.6 11.9 %collective-permute-start = (bf16[1024,128]{1,0:T(8,128)(2,1)}, bf16[1024,128]{1,0:T(8,128)(2,1)S(1)}, u32[]{:S(2)}, u32[]{:S(2)}) collective-permute-start(bf16[1024,128]{1,0:T(8,128)(2,1)} %items.1), channel_id=1, source_target_pairs={{0,24},{1,29},{2,26},{3,31},{4,28},{5,1},{6,30},{7,3},{8,0},{9,5},... | collective-permute-start | bytes 786440 | tf_op jit(solution)/shard_map/ppermute | solution.py:249
  9.0 9.5 %collective-permute-start.2 = (f32[4,128,128]{2,1,0:T(8,128)}, f32[4,128,128]{2,1,0:T(8,128)S(1)}, u32[]{:S(2)}, u32[]{:S(2)}) collective-permute-start(f32[4,128,128]{2,1,0:T(8,128)} %constant_dynamic-slice_fusion), channel_id=1, source_target_pairs={{0,1},{1,0},{2,3},{3,2},{4,5},{5,4},{6,7},{7,6},{8,9},{9,8},{10,11... | collective-permute-start | bytes 786440 | tf_op jit(solution)/shard_map/ppermute | solution.py:253
  12.6 2.0 %collective-permute-start.1 = (bf16[1024,128]{1,0:T(8,128)(2,1)S(1)}, bf16[1024,128]{1,0:T(8,128)(2,1)S(1)}, u32[]{:S(2)}, u32[]{:S(2)}) collective-permute-start(bf16[1024,128]{1,0:T(8,128)(2,1)S(1)} %collective-permute-done.refs_5_), channel_id=1, source_target_pairs={{0,1},{1,0},{2,3},{3,2},{4,5},{5,4},{6,7},{7,6},{8,9},{9,8},{10,11... | collective-permute-start | bytes 786440 | tf_op jit(solution)/shard_map/ppermute | solution.py:253
  14.2 2.1 %collective-permute-start.3 = (f16[8,128,128]{2,1,0:T(8,128)(2,1)S(1)}, f16[8,128,128]{2,1,0:T(8,128)(2,1)S(1)}, u32[]{:S(2)}, u32[]{:S(2)}) collective-permute-start(f16[8,128,128]{2,1,0:T(8,128)(2,1)S(1)} %multiply_convert_fusion), channel_id=1, source_target_pairs={{0,1},{1,0},{2,3},{3,2},{4,5},{5,4},{6,7},{7,6},{8,9},{9,8},{10,11... | collective-permute-start | bytes 786440 | tf_op jit(solution)/shard_map/ppermute | solution.py:253
  16.4 14.8 %copy-start = (bf16[1024,128]{1,0:T(8,128)(2,1)S(1)}, bf16[1024,128]{1,0:T(8,128)(2,1)}, u32[]{:S(2)}) copy-start(bf16[1024,128]{1,0:T(8,128)(2,1)} %items.1) | copy-start | bytes 786436
  16.4 9.1 %collective-permute-start.4 = (f16[4,128,128]{2,1,0:T(8,128)(2,1)S(1)}, f16[4,128,128]{2,1,0:T(8,128)(2,1)S(1)}, u32[]{:S(2)}, u32[]{:S(2)}) collective-permute-start(f16[4,128,128]{2,1,0:T(8,128)(2,1)S(1)} %get-tuple-element.28), channel_id=1, source_target_pairs={{0,4},{1,9},{2,6},{3,11},{4,8},{5,13},{6,10},{7,15},{8,12},{9,17},... | collective-permute-start | bytes 393224 | tf_op jit(solution)/shard_map/ppermute | solution.py:249
  16.5 9.0 %collective-permute-start.5 = (f16[4,128,128]{2,1,0:T(8,128)(2,1)S(1)}, f16[4,128,128]{2,1,0:T(8,128)(2,1)S(1)}, u32[]{:S(2)}, u32[]{:S(2)}) collective-permute-start(f16[4,128,128]{2,1,0:T(8,128)(2,1)S(1)} %get-tuple-element.29), channel_id=1, source_target_pairs={{0,5},{1,8},{2,7},{3,10},{4,9},{5,12},{6,11},{7,14},{8,13},{9,16},... | collective-permute-start | bytes 393224 | tf_op jit(solution)/shard_map/ppermute | solution.py:249
  25.6 5.4 %collective-permute-start.6 = (f16[4,128,128]{2,1,0:T(8,128)(2,1)S(1)}, f16[4,128,128]{2,1,0:T(8,128)(2,1)S(1)}, u32[]{:S(2)}, u32[]{:S(2)}) collective-permute-start(f16[4,128,128]{2,1,0:T(8,128)(2,1)S(1)} %multiply_convert_fusion.1), channel_id=1, source_target_pairs={{0,2},{1,3},{2,0},{3,1},{4,6},{5,7},{6,4},{7,5},{8,10},{9,11},{10,... | collective-permute-start | bytes 393224 | tf_op jit(solution)/shard_map/ppermute | solution.py:253
  31.2 1.9 %collective-permute-start.7 = (bf16[512,128]{1,0:T(8,128)(2,1)S(1)}, bf16[512,128]{1,0:T(8,128)(2,1)S(1)}, u32[]{:S(2)}, u32[]{:S(2)}) collective-permute-start(bf16[512,128]{1,0:T(8,128)(2,1)S(1)} %fusion.5), channel_id=1, source_target_pairs={{0,1},{1,0},{2,3},{3,2},{4,5},{5,4},{6,7},{7,6},{8,9},{9,8},{10,11... | collective-permute-start | bytes 393224 | tf_op jit(solution)/shard_map/ppermute | solution.py:253

commit v5 on v4

--- a/solution.py
+++ b/solution.py
@@ -32,11 +32,11 @@
 
 
 def near_stop(core):
+    return 1 + core
+
+
+def far_stop(core):
     return 2 - core
-
-
-def far_stop(core):
-    return 1 + core
 
 
 def steps(live, size):

time: 34.5 us -> 35.6 us (1.032); the launches traced: 33.9 us -> 35.7 us
  waiting for transfers between devices: 13.6 us -> 18.4 us
  starting transfers between devices: 11 us -> 6.67 us
  Pallas kernels: 5.79 us -> 7 us
    ppermute x3, waiting for transfers between devices: 9.61 us -> 13 us  [joint(): return lax.ppermute(block, ('blk', 'rep'), route)]
    ppermute x5, starting transfers between devices: 3.83 us -> 0.49 us  [swap(): lax.ppermute(block, 'rep', [(r, r ^ bit) for r in range(lax.axis_size('re...]
    ppermute x5, waiting for transfers between devices: 3.94 us -> 5.48 us  [swap(): lax.ppermute(block, 'rep', [(r, r ^ bit) for r in range(lax.axis_size('re...]
    pallas_call x2, Pallas kernels: 3.25 us -> 4.3 us  [stop_call(): pl.pallas_call(functools.partial(stop_kernel, which, following), out_shap...]
    ppermute x3, starting transfers between devices: 7.19 us -> 6.17 us  [joint(): return lax.ppermute(block, ('blk', 'rep'), route)]
  transfers between devices with their start and end apart: 8 -> 8, of which waited for: 4 -> 5; matrix products, arithmetic and copies ran while one was open for 5% -> 5% of each run, Pallas kernels for 17% -> 20%
where the time goes in v5:
time: 35.6 us; the launch traced here: 35.7 us
  waiting for transfers between devices  18.4 us (52%)
  Pallas kernels  7 us (20%)
  starting transfers between devices  6.67 us (19%)
  other arithmetic  1.95 us (5%)
  local copies, waits for them, and re-layouts  0.86 us (2%)
  between operations  0.78 us (2%)
    ppermute x3, waiting for transfers between devices, joint(): return lax.ppermute(block, ('blk', 'rep'), route)  13 us
    ppermute x3, starting transfers between devices, joint(): return lax.ppermute(block, ('blk', 'rep'), route)  6.17 us
    ppermute x5, waiting for transfers between devices, swap(): lax.ppermute(block, 'rep', [(r, r ^ bit) for r in range(lax.axis_size('re...  5.48 us
    pallas_call x2, Pallas kernels, stop_call(): pl.pallas_call(functools.partial(stop_kernel, which, following), out_shap...  4.3 us
    pallas_call x1, Pallas kernels, own_call(): pl.pallas_call(own_kernel, out_shape=(shape(users.shape, f32), shape((n_i...  2.7 us
    convert_element_type x1, other arithmetic, on_device(): (users32 - rate_user * (total + shrinkage * users32)).astype(users.dtype)  0.81 us
    dynamic_slice x1, local copies, waits for them, and re-layouts, half_of(): return lax.dynamic_slice_in_dim(array, c * half, half)  0.73 us
    concatenate x1, other arithmetic, on_device(): return (user_new, jnp.concatenate([low, high]))  0.72 us
  transfers between devices with their start and end apart: 8, of which 5 were waited for; matrix products, arithmetic and copies ran while one was open for 5% of the time, Pallas kernels for 20%

profile of v5, /device:TPU:0, one launch (start us, length us, event | category | flops | bytes accessed | tf_op | source)
XLA Modules:
  0.0 35.7 jit_solution(1829547133630408617)
XLA Ops:
  0.6 6.1 %collective-permute-start = (bf16[1024,128]{1,0:T(8,128)(2,1)}, bf16[1024,128]{1,0:T(8,128)(2,1)S(1)}, u32[]{:S(2)}, u32[]{:S(2)}) collective-permute-start(bf16[1024,128]{1,0:T(8,128)(2,1)} %items.1), channel_id=1, source_target_pairs={{0,28},{1,25},{2,30},{3,27},{4,0},{5,29},{6,2},{7,31},{8,4},{9,1},... | collective-permute-start | bytes 786440 | tf_op jit(solution)/shard_map/ppermute | solution.py:249
  6.7 2.7 %shard_map.77 = (f32[1024,128]{1,0:T(8,128)S(1)}, f32[8,128,128]{2,1,0:T(8,128)S(1)}, bf16[40,128,128]{2,1,0:T(8,128)(2,1)S(1)}, bf16[1024,128]{1,0:T(8,128)(2,1...) custom-call(s32[1,1,3]{2,1,0:T(1,128)} %counts.1, ...), custom_call_target="tpu_custom_call" | custom-call | flops 10000000000 | bytes 8000000 | tf_op jit(solution)/shard_map/pallas_call | solution.py:154
  9.4 0.7 %constant_dynamic-slice_fusion = f32[4,128,128]{2,1,0:T(8,128)} fusion(f32[8,128,128]{2,1,0:T(8,128)S(1)} %get-tuple-element.25, s32[]{:T(128)S(6)} %select_n.26), kind=kLoop, calls=%fused_computation.19 | loop fusion | bytes 524292 | tf_op jit(solution)/shard_map/dynamic_slice | solution.py:281
  10.1 0.0 collective-permute-start.2
  10.1 1.5 %collective-permute-done.refs_5_ = bf16[1024,128]{1,0:T(8,128)(2,1)S(1)} collective-permute-done((bf16[1024,128]{1,0:T(8,128)(2,1)}, bf16[1024,128]{1,0:T(8,128)(2,1)S(1)}, u32[]{:S(2)}, u32[]{:S(2)}) %collective-permute-start) | collective-permute-done | bytes 262176 | tf_op jit(solution)/shard_map/ppermute | solution.py:249
  11.6 0.0 collective-permute-start.1
  11.6 1.6 %shard_map.78 = (f32[1024,128]{1,0:T(8,128)S(1)}, f32[8,128,128]{2,1,0:T(8,128)S(1)}, bf16[40,128,128]{2,1,0:T(8,128)(2,1)S(1)}) custom-call(s32[1,1,3]{2,1,0:T(1,128)S(1)} %get-tuple-element.16.refs_0_, s32[1,3,1,40]{3,2,1,0:T(1,128)S(1)} %get-tuple-element.17.refs_1_, ...), custom_call_target="tpu_custom_call", output_to_operand_aliasing={{0}: (7, {})} | custom-call | flops 10000000000 | bytes 8000000 | tf_op jit(solution)/shard_map/pallas_call | solution.py:230
  13.2 0.1 multiply_convert_fusion
  13.3 0.3 collective-permute-start.3
  13.6 0.0 collective-permute-done.1.refs_5_
  13.6 2.7 %shard_map.79 = (f32[1024,128]{1,0:T(8,128)S(1)}, f32[8,128,128]{2,1,0:T(8,128)S(1)}) custom-call(s32[1,1,3]{2,1,0:T(1,128)S(1)} %get-tuple-element.16.refs_0_, s32[1,3,1,40]{3,2,1,0:T(1,128)S(1)} %get-tuple-element.17.refs_1_, s32[1,3,1,40]{3,2,1,0:T(1,128)S(1)} %get-tuple-element.18.refs_2_, ...), custom_call_target="tpu_custom_call", output_to_operand_aliasing={{0}: (7, {})} | custom-call | flops 10000000000 | bytes 8000000 | tf_op jit(solution)/shard_map/pallas_call | solution.py:230
  16.3 0.0 collective-permute-done.3
  16.4 0.1 multiply_add_fusion
  16.4 0.0 copy-start
  16.5 0.1 multiply_convert_fusion.3
  16.5 0.1 collective-permute-start.4
  16.6 0.1 collective-permute-start.5
  16.7 0.0 collective-permute-done.2
  16.7 6.7 %collective-permute-done.4 = f16[4,128,128]{2,1,0:T(8,128)(2,1)S(1)} collective-permute-done((f16[4,128,128]{2,1,0:T(8,128)(2,1)S(1)}, f16[4,128,128]{2,1,0:T(8,128)(2,1)S(1)}, u32[]{:S(2)}, u32[]{:S(2)}) %collective-permute-start.4) | collective-permute-done | bytes 131104 | tf_op jit(solution)/shard_map/ppermute | solution.py:249
  23.3 4.8 %collective-permute-done.5 = f16[4,128,128]{2,1,0:T(8,128)(2,1)S(1)} collective-permute-done((f16[4,128,128]{2,1,0:T(8,128)(2,1)S(1)}, f16[4,128,128]{2,1,0:T(8,128)(2,1)S(1)}, u32[]{:S(2)}, u32[]{:S(2)}) %collective-permute-start.5) | collective-permute-done | bytes 131104 | tf_op jit(solution)/shard_map/ppermute | solution.py:249
  28.2 0.1 multiply_convert_fusion.1
  28.3 0.1 collective-permute-start.6
  28.3 4.9 %collective-permute-done.6 = f16[4,128,128]{2,1,0:T(8,128)(2,1)S(1)} collective-permute-done((f16[4,128,128]{2,1,0:T(8,128)(2,1)S(1)}, f16[4,128,128]{2,1,0:T(8,128)(2,1)S(1)}, u32[]{:S(2)}, u32[]{:S(2)}) %collective-permute-start.6) | collective-permute-done | bytes 131104 | tf_op jit(solution)/shard_map/ppermute | solution.py:253
  33.3 0.1 copy.10
  33.5 0.0 copy-done
  33.5 0.1 fusion.5
  33.5 0.1 collective-permute-start.7
  33.6 0.8 %fusion.2 = bf16[1024,128]{1,0:T(8,128)(2,1)} fusion(f32[1024,128]{1,0:T(8,128)S(1)} %get-tuple-element.24, bf16[1024,128]{1,0:T(8,128)(2,1)S(1)} %get-tuple-element.15.refs_3_), kind=kLoop, calls=%fused_computation.4 | loop fusion | flops 786432 | bytes 1048576 | tf_op jit(solution)/shard_map/convert_element_type | solution.py:276
  34.4 0.5 %collective-permute-done.7 = bf16[512,128]{1,0:T(8,128)(2,1)S(1)} collective-permute-done((bf16[512,128]{1,0:T(8,128)(2,1)S(1)}, bf16[512,128]{1,0:T(8,128)(2,1)S(1)}, u32[]{:S(2)}, u32[]{:S(2)}) %collective-permute-start.7) | collective-permute-done | bytes 131104 | tf_op jit(solution)/shard_map/ppermute | solution.py:253
  35.0 0.7 %pad_maximum_fusion = bf16[1024,128]{1,0:T(8,128)(2,1)} fusion(bf16[512,128]{1,0:T(8,128)(2,1)S(1)} %get-tuple-element.31, bf16[512,128]{1,0:T(8,128)(2,1)S(1)} %get-tuple-element.30), kind=kLoop, calls=%fused_computation.12 | loop fusion | flops 524288 | bytes 524288 | tf_op jit(solution)/shard_map/concatenate | solution.py:299
  (2 shorter events, 0.1 us)
Async XLA Ops:
  0.6 11.0 %collective-permute-start = (bf16[1024,128]{1,0:T(8,128)(2,1)}, bf16[1024,128]{1,0:T(8,128)(2,1)S(1)}, u32[]{:S(2)}, u32[]{:S(2)}) collective-permute-start(bf16[1024,128]{1,0:T(8,128)(2,1)} %items.1), channel_id=1, source_target_pairs={{0,28},{1,25},{2,30},{3,27},{4,0},{5,29},{6,2},{7,31},{8,4},{9,1},... | collective-permute-start | bytes 786440 | tf_op jit(solution)/shard_map/ppermute | solution.py:249
  10.1 6.5 %collective-permute-start.2 = (f32[4,128,128]{2,1,0:T(8,128)}, f32[4,128,128]{2,1,0:T(8,128)S(1)}, u32[]{:S(2)}, u32[]{:S(2)}) collective-permute-start(f32[4,128,128]{2,1,0:T(8,128)} %constant_dynamic-slice_fusion), channel_id=1, source_target_pairs={{0,1},{1,0},{2,3},{3,2},{4,5},{5,4},{6,7},{7,6},{8,9},{9,8},{10,11... | collective-permute-start | bytes 786440 | tf_op jit(solution)/shard_map/ppermute | solution.py:253
  11.6 2.0 %collective-permute-start.1 = (bf16[1024,128]{1,0:T(8,128)(2,1)S(1)}, bf16[1024,128]{1,0:T(8,128)(2,1)S(1)}, u32[]{:S(2)}, u32[]{:S(2)}) collective-permute-start(bf16[1024,128]{1,0:T(8,128)(2,1)S(1)} %collective-permute-done.refs_5_), channel_id=1, source_target_pairs={{0,1},{1,0},{2,3},{3,2},{4,5},{5,4},{6,7},{7,6},{8,9},{9,8},{10,11... | collective-permute-start | bytes 786440 | tf_op jit(solution)/shard_map/ppermute | solution.py:253
  13.3 3.1 %collective-permute-start.3 = (f16[8,128,128]{2,1,0:T(8,128)(2,1)S(1)}, f16[8,128,128]{2,1,0:T(8,128)(2,1)S(1)}, u32[]{:S(2)}, u32[]{:S(2)}) collective-permute-start(f16[8,128,128]{2,1,0:T(8,128)(2,1)S(1)} %multiply_convert_fusion), channel_id=1, source_target_pairs={{0,1},{1,0},{2,3},{3,2},{4,5},{5,4},{6,7},{7,6},{8,9},{9,8},{10,11... | collective-permute-start | bytes 786440 | tf_op jit(solution)/shard_map/ppermute | solution.py:253
  16.4 17.0 %copy-start = (bf16[1024,128]{1,0:T(8,128)(2,1)S(1)}, bf16[1024,128]{1,0:T(8,128)(2,1)}, u32[]{:S(2)}) copy-start(bf16[1024,128]{1,0:T(8,128)(2,1)} %items.1) | copy-start | bytes 786436
  16.5 6.8 %collective-permute-start.4 = (f16[4,128,128]{2,1,0:T(8,128)(2,1)S(1)}, f16[4,128,128]{2,1,0:T(8,128)(2,1)S(1)}, u32[]{:S(2)}, u32[]{:S(2)}) collective-permute-start(f16[4,128,128]{2,1,0:T(8,128)(2,1)S(1)} %get-tuple-element.28), channel_id=1, source_target_pairs={{0,8},{1,5},{2,10},{3,7},{4,12},{5,9},{6,14},{7,11},{8,16},{9,13},... | collective-permute-start | bytes 393224 | tf_op jit(solution)/shard_map/ppermute | solution.py:249
  16.6 11.6 %collective-permute-start.5 = (f16[4,128,128]{2,1,0:T(8,128)(2,1)S(1)}, f16[4,128,128]{2,1,0:T(8,128)(2,1)S(1)}, u32[]{:S(2)}, u32[]{:S(2)}) collective-permute-start(f16[4,128,128]{2,1,0:T(8,128)(2,1)S(1)} %get-tuple-element.29), channel_id=1, source_target_pairs={{0,9},{1,4},{2,11},{3,6},{4,13},{5,8},{6,15},{7,10},{8,17},{9,12},... | collective-permute-start | bytes 393224 | tf_op jit(solution)/shard_map/ppermute | solution.py:249
  28.3 5.0 %collective-permute-start.6 = (f16[4,128,128]{2,1,0:T(8,128)(2,1)S(1)}, f16[4,128,128]{2,1,0:T(8,128)(2,1)S(1)}, u32[]{:S(2)}, u32[]{:S(2)}) collective-permute-start(f16[4,128,128]{2,1,0:T(8,128)(2,1)S(1)} %multiply_convert_fusion.1), channel_id=1, source_target_pairs={{0,2},{1,3},{2,0},{3,1},{4,6},{5,7},{6,4},{7,5},{8,10},{9,11},{10,... | collective-permute-start | bytes 393224 | tf_op jit(solution)/shard_map/ppermute | solution.py:253
  33.5 1.4 %collective-permute-start.7 = (bf16[512,128]{1,0:T(8,128)(2,1)S(1)}, bf16[512,128]{1,0:T(8,128)(2,1)S(1)}, u32[]{:S(2)}, u32[]{:S(2)}) collective-permute-start(bf16[512,128]{1,0:T(8,128)(2,1)S(1)} %fusion.5), channel_id=1, source_target_pairs={{0,1},{1,0},{2,3},{3,2},{4,5},{5,4},{6,7},{7,6},{8,9},{9,8},{10,11... | collective-permute-start | bytes 393224 | tf_op jit(solution)/shard_map/ppermute | solution.py:253
